TPU v7x, 32 devices: a whole 2x2x4 slice. The times are simulated.
32 devices in a mesh: space: 8 (over y, x, core), chaos: 4 (over z).
Axes of the slice: x: 2, y: 2, z: 4, core: 2. Of those that a mesh axis runs over, the one named last changes fastest.
Arguments:
- field: bfloat16 [168, 131072], P('chaos', 'space'), may hold values from -6 to 6
- stiffness: bfloat16 [2048, 4096], P(('space', 'chaos')), may hold values from -0.75 to 0.75
- kl_coef: float32 [9, 2048], P(None, ('space', 'chaos')), may hold values from -3 to 3
- triple_mode: int32 [2688], replicated, may hold values from 0 to 7
- triple_row: int32 [2688], replicated, may hold values from 0 to 167
- triple_col: int32 [2688], replicated, may hold values from 0 to 167
- triple_value: float32 [2688], replicated, may hold values from -3 to 3
- die_elem: int32 [4096], P(('space', 'chaos')), may hold values from 0 to 63
- die_side: int32 [4096], P(('space', 'chaos')), may hold values from 0 to 5
- seg_owner: int32 [4096], P(('space', 'chaos')), may hold values from 0 to 31, as said below
- seg_face: int32 [4096], P(('space', 'chaos')), may hold values from 0 to 63
- die_mortar: bfloat16 [4096, 256], P(('space', 'chaos')), may hold values from -1.5 to 1.5
- int_mortar: bfloat16 [4096, 256], P(('space', 'chaos')), may hold values from -1.5 to 1.5
- bump_coef: bfloat16 [4096, 9], P(('space', 'chaos')), may hold values from -3 to 3
- int_elem: int32 [2048], P(('space', 'chaos')), may hold values from 0 to 63
- int_side: int32 [2048], P(('space', 'chaos')), may hold values from 0 to 5
Outputs:
- response: bfloat16 [168, 131072], P('chaos', 'space')
Inputs may be any that keep to these rules, and one draw needn't show every extreme that they name: `seg_owner`: in each device's block of 128 segments no owner appears more than 8 times; one owner device receives exactly 8 segments from every device's block.
All inputs are finite; a program needn't handle non-finite values.
Results may differ from a plain program's by a relative error of at most 0.006.
Values may be sent and summed in bfloat16 or wider, within the bound.
A program may use at most 64 MiB of HBM per device.

v0:
```python
import jax
import jax.numpy as jnp
import numpy as np
from jax import lax
from jax.sharding import PartitionSpec as P

P_SIZE = 168
MODES = 8
ELEM_NODES = 64


def face_nodes():
    node_rows = []
    for side_idx in range(6):
        normal_axis = side_idx // 2
        plane_level = 3 * (side_idx % 2)
        row_nodes = []
        for first_coord in range(4):
            for second_coord in range(4):
                position = [first_coord, second_coord]
                position.insert(normal_axis, plane_level)
                row_nodes.append(16 * position[0] + 4 * position[1] + position[2])
        node_rows.append(row_nodes)
    return np.array(node_rows, dtype=np.int32)


def side_nodes(side_ids):
    node_table = jnp.asarray(face_nodes())
    side_hot = (side_ids[:, None] == jnp.arange(6, dtype=jnp.int32)[None, :]).astype(jnp.int32)
    return jnp.sum(side_hot[:, :, None] * node_table[None, :, :], axis=1)


def dense_coupling(triple_mode, triple_row, triple_col, triple_value, mode_count, chaos_width):
    flat_index = triple_mode * chaos_width + triple_row
    left_hot = (
        flat_index[:, None] == jnp.arange(mode_count * chaos_width, dtype=jnp.int32)[None, :]
    ).astype(jnp.float32)
    right_hot = (triple_col[:, None] == jnp.arange(chaos_width, dtype=jnp.int32)[None, :]).astype(
        jnp.float32
    ) * triple_value[:, None]
    summed = jnp.einsum(
        "ta,tb->ab",
        left_hot,
        right_hot,
        precision=lax.Precision.HIGHEST,
        preferred_element_type=jnp.float32,
    )
    return summed.reshape(mode_count, chaos_width, chaos_width).astype(jnp.bfloat16)


def mix_flux(jump_vals, coef_rows, coupling):
    chaos_width = jump_vals.shape[2]
    flat_jump = jump_vals.reshape(-1, chaos_width)
    weights = coef_rows.astype(jnp.float32)
    accum = weights[:, 0][:, None, None] * jump_vals.astype(jnp.float32)
    for mode_idx in range(coupling.shape[0]):
        term = jnp.einsum(
            "rj,ij->ri", flat_jump, coupling[mode_idx], preferred_element_type=jnp.float32
        ).reshape(jump_vals.shape)
        accum = accum + weights[:, mode_idx + 1][:, None, None] * term
    return accum.astype(jnp.bfloat16)


def local(
    field,
    stiffness,
    kl_coef,
    triple_mode,
    triple_row,
    triple_col,
    triple_value,
    die_elem,
    die_side,
    seg_owner,
    seg_face,
    die_mortar,
    int_mortar,
    bump_coef,
    int_elem,
    int_side,
):
    coupling = dense_coupling(triple_mode, triple_row, triple_col, triple_value, MODES, P_SIZE)
    local_field = lax.all_to_all(field, "chaos", split_axis=1, concat_axis=0, tiled=True)
    chaos_width = local_field.shape[0]
    node_count = local_field.shape[1]
    elements = node_count // ELEM_NODES
    kl_nodes = jnp.repeat(kl_coef, ELEM_NODES, axis=1)
    mixed = kl_nodes[0] * local_field.astype(jnp.float32)
    for mode_idx in range(MODES):
        mixed = mixed + kl_nodes[mode_idx + 1] * jnp.dot(
            coupling[mode_idx], local_field, preferred_element_type=jnp.float32
        )
    mixed = mixed.astype(jnp.bfloat16)
    mixed_blocks = jnp.transpose(mixed.reshape(chaos_width, elements, ELEM_NODES), (1, 0, 2))
    blocks = stiffness.reshape(elements, ELEM_NODES, ELEM_NODES)
    local_out = jnp.einsum("epb,eab->epa", mixed_blocks, blocks, preferred_element_type=jnp.float32)
    die_nodes = die_elem[:, None] * ELEM_NODES + side_nodes(die_side)
    die_mats = die_mortar.reshape(-1, 16, 16)
    die_face = local_field[:, die_nodes]
    die_proj = jnp.einsum(
        "sgf,psf->sgp", die_mats, die_face, preferred_element_type=jnp.float32
    ).astype(jnp.bfloat16)
    n_space = lax.axis_size("space")
    n_chaos = lax.axis_size("chaos")
    device_total = n_space * n_chaos
    seg_count = die_elem.shape[0]
    capacity = max(2, 2 * seg_count // device_total)
    slot_total = device_total * capacity
    owner_hot = (seg_owner[:, None] == jnp.arange(device_total, dtype=jnp.int32)[None, :]).astype(
        jnp.int32
    )
    earlier = jnp.cumsum(owner_hot, axis=0) - owner_hot
    slot_index = seg_owner * capacity + jnp.sum(earlier * owner_hot, axis=1)
    send_proj = (
        jnp.zeros((slot_total, 16 * chaos_width), jnp.bfloat16)
        .at[slot_index]
        .set(die_proj.reshape(seg_count, 16 * chaos_width))
    )
    send_mats = jnp.zeros((slot_total, 256), jnp.bfloat16).at[slot_index].set(int_mortar)
    send_coef = (
        jnp.zeros((slot_total, bump_coef.shape[1]), jnp.bfloat16).at[slot_index].set(bump_coef)
    )
    send_face = jnp.zeros((slot_total,), jnp.int32).at[slot_index].set(seg_face)
    recv_proj, recv_mats, recv_coef, recv_face = (
        lax.all_to_all(send_proj, ("space", "chaos"), split_axis=0, concat_axis=0, tiled=True),
        lax.all_to_all(send_mats, ("space", "chaos"), split_axis=0, concat_axis=0, tiled=True),
        lax.all_to_all(send_coef, ("space", "chaos"), split_axis=0, concat_axis=0, tiled=True),
        lax.all_to_all(send_face, ("space", "chaos"), split_axis=0, concat_axis=0, tiled=True),
    )
    own_elem = int_elem[recv_face]
    own_side = int_side[recv_face]
    own_corner = side_nodes(own_side)
    own_nodes = own_elem[:, None] * ELEM_NODES + own_corner
    own_mats = recv_mats.reshape(-1, 16, 16)
    own_face = local_field[:, own_nodes]
    own_proj = jnp.einsum("rgf,prf->rgp", own_mats, own_face, preferred_element_type=jnp.float32)
    jump_vals = (
        recv_proj.reshape(slot_total, 16, chaos_width).astype(jnp.float32) - own_proj
    ).astype(jnp.bfloat16)
    jump_vals = lax.optimization_barrier(jump_vals)
    seg_flux = mix_flux(jump_vals, recv_coef, coupling)
    own_back = jnp.einsum(
        "rgf,rgp->rfp", own_mats, seg_flux, preferred_element_type=jnp.float32
    ).reshape(-1, chaos_width)
    own_elem_rows = jnp.repeat(own_elem, 16)
    local_out = local_out.at[own_elem_rows, :, own_corner.reshape(-1)].add(-own_back)
    flux_slots = seg_flux.reshape(slot_total, 16 * chaos_width)
    back_flux = lax.all_to_all(
        flux_slots, ("space", "chaos"), split_axis=0, concat_axis=0, tiled=True
    )
    die_flux = back_flux[slot_index].reshape(seg_count, 16, chaos_width)
    die_back = jnp.einsum(
        "sgf,sgp->sfp", die_mats, die_flux, preferred_element_type=jnp.float32
    ).reshape(-1, chaos_width)
    die_elem_rows = jnp.repeat(die_elem, 16)
    die_corner = side_nodes(die_side).reshape(-1)
    local_out = local_out.at[die_elem_rows, :, die_corner].add(die_back)
    result = local_out.astype(jnp.bfloat16)
    returned = lax.all_to_all(result, "chaos", split_axis=1, concat_axis=0, tiled=True)
    term_count = returned.shape[1]
    return jnp.transpose(returned, (1, 0, 2)).reshape(term_count, -1)


def solution(mesh):
    in_specs = (
        P("chaos", "space"),
        P(("space", "chaos"), None),
        P(None, ("space", "chaos")),
        P(),
        P(),
        P(),
        P(),
        P(("space", "chaos")),
        P(("space", "chaos")),
        P(("space", "chaos")),
        P(("space", "chaos")),
        P(("space", "chaos"), None),
        P(("space", "chaos"), None),
        P(("space", "chaos"), None),
        P(("space", "chaos")),
        P(("space", "chaos")),
    )
    out_specs = P("chaos", "space")
    return jax.shard_map(local, mesh=mesh, in_specs=in_specs, out_specs=out_specs, check_vma=False)
```

profile of v0, /device:TPU:0, one launch (start us, length us, event | category | flops | bytes accessed | tf_op | source)
XLA Modules:
  0.0 311.8 jit_solution(9246873120991156801)
XLA Ops:
  4.2 7.3 %all-to-all-start.1 = ((s32[32,8,1]{1,2,0:T(1,128)}), s32[32,8,1]{1,2,0:T(1,128)S(1)}, u32[]{:S(2)}, u32[]{:S(2)}) async-start(s32[32,8,1]{1,2,0:T(1,128)} %bitcast.14), calls=%async_computation.1 | async-start | bytes 32768 | tf_op jit(solution)/shard_map/all_to_all | solution.py:128
  20.2 5.0 %all-to-all-start = ((bf16[42,4,4096]{2,0,1:T(8,128)(2,1)}), bf16[42,4,4096]{2,0,1:T(8,128)(2,1)S(1)}, u32[]{:S(2)}, u32[]{:S(2)}) async-start(bf16[42,4,4096]{2,0,1:T(8,128)(2,1)} %copy.224), calls=%async_computation | async-start | bytes 3145728 | tf_op jit(solution)/shard_map/all_to_all | solution.py:83
  40.6 7.7 %fusion.12 = bf16[1344,168]{0,1:T(8,128)(2,1)} fusion(s32[2688]{0:T(1024)S(1)} %multiply_add_fusion, f32[2688]{0:T(1024)S(1)} %copy-done.33, s32[2688]{0:T(1024)S(1)} %copy-done.34), kind=kOutput, calls=%fused_computation.35 | convolution fusion | flops 7287888384 | bytes 483840 | tf_op jit(solution)/shard_map/ta,tb->ab/dot_general | solution.py:41
  54.0 8.5 %all-to-all-done = bf16[42,4,4096]{2,0,1:T(8,128)(2,1)S(1)} async-done(((bf16[42,4,4096]{2,0,1:T(8,128)(2,1)}), bf16[42,4,4096]{2,0,1:T(8,128)(2,1)S(1)}, u32[]{:S(2)}, u32[]{:S(2)}) %all-to-all-start) | async-done | bytes 1376288 | tf_op jit(solution)/shard_map/all_to_all | solution.py:83
  62.5 3.7 %all-to-all-start.3 = ((bf16[32,8,9]{2,1,0:T(8,128)(2,1)}), bf16[32,8,9]{2,1,0:T(8,128)(2,1)S(1)}, u32[]{:S(2)}, u32[]{:S(2)}) async-start(bf16[32,8,9]{2,1,0:T(8,128)(2,1)} %bitcast.17), calls=%async_computation.3 | async-start | bytes 131072 | tf_op jit(solution)/shard_map/all_to_all | solution.py:127
  69.1 9.1 %gather_fusion.2 = bf16[2048,168]{1,0:T(8,128)(2,1)} fusion(bf16[168,4096]{0,1:T(8,128)(2,1)S(1)} %copy.232, s32[2048]{0:T(1024)S(1)} %broadcast_clamp_fusion.1), kind=kCustom, calls=%fused_computation.2 | custom fusion | bytes 1384448 | tf_op jit(solution)/shard_map/gather | solution.py:99
  78.2 6.0 %all-to-all-start.2 = ((bf16[32,8,256]{2,1,0:T(8,128)(2,1)}), bf16[32,8,256]{2,1,0:T(8,128)(2,1)}, u32[]{:S(2)}, u32[]{:S(2)}) async-start(bf16[32,8,256]{2,1,0:T(8,128)(2,1)} %bitcast.146), calls=%async_computation.2 | async-start | bytes 262144 | tf_op jit(solution)/shard_map/all_to_all | solution.py:126
  95.2 6.0 %all-to-all-start.4 = ((bf16[32,8,2688]{2,1,0:T(8,128)(2,1)}), bf16[32,8,2688]{2,1,0:T(8,128)(2,1)}, u32[]{:S(2)}, u32[]{:S(2)}) async-start(bf16[32,8,2688]{2,1,0:T(8,128)(2,1)} %bitcast.142), calls=%async_computation.4 | async-start | bytes 2752512 | tf_op jit(solution)/shard_map/all_to_all | solution.py:125
  111.4 17.1 %gather_fusion.3 = bf16[4096,168]{1,0:T(8,128)(2,1)} fusion(bf16[168,4096]{0,1:T(8,128)(2,1)S(1)} %copy.232, s32[4096]{0:T(1024)S(1)} %broadcast_clamp_fusion), kind=kCustom, calls=%fused_computation.3 | custom fusion | bytes 2768896 | tf_op jit(solution)/shard_map/gather | solution.py:135
  128.4 4.5 %fusion.64 = f32[256,16,168]{2,1,0:T(8,128)} fusion(bf16[256,16,16]{2,1,0:T(8,128)(2,1)} %reshape.424, bf16[168,256,16]{0,2,1:T(8,128)(2,1)} %bitcast.132), kind=kOutput, calls=%fused_computation.127 | convolution fusion | flops 22020096 | bytes 4259840 | tf_op jit(solution)/shard_map/rgf,prf->rgp/dot_general | solution.py:136
  133.0 5.1 %copy.240 = f32[256,16,168]{0,2,1:T(8,128)} copy(f32[256,16,168]{2,1,0:T(8,128)} %fusion.64) | data formatting | bytes 5505024 | tf_op jit(solution)/shard_map/rgf,prf->rgp/dot_general | solution.py:136
  141.8 7.8 %reshape.442 = f32[256,16,168]{2,1,0:T(8,128)} reshape(bf16[32,8,2688]{2,1,0:T(8,128)(2,1)} %all-to-all-done.4) | data formatting | bytes 4128768 | tf_op jit(solution)/shard_map/convert_element_type | solution.py:138
  149.5 5.0 %copy.239 = f32[256,16,168]{0,2,1:T(8,128)} copy(f32[256,16,168]{2,1,0:T(8,128)} %reshape.442) | data formatting | bytes 5505024 | tf_op jit(solution)/shard_map/convert_element_type | solution.py:138
  168.8 4.4 %all_to_all.74 = bf16[32,8,2688]{2,1,0:T(8,128)(2,1)} reshape(bf16[256,16,168]{2,1,0:T(8,128)(2,1)S(1)} %copy.250) | data formatting | bytes 2752512 | tf_op jit(solution)/shard_map/all_to_all | solution.py:148
  173.2 5.9 %all-to-all-start.5 = ((bf16[32,8,2688]{2,1,0:T(8,128)(2,1)}), bf16[32,8,2688]{2,1,0:T(8,128)(2,1)S(1)}, u32[]{:S(2)}, u32[]{:S(2)}) async-start(bf16[32,8,2688]{2,1,0:T(8,128)(2,1)} %all_to_all.74), calls=%async_computation.5 | async-start | bytes 2752512 | tf_op jit(solution)/shard_map/all_to_all | solution.py:148
  185.7 3.8 %copy.225 = bf16[168,4096]{0,1:T(8,128)(2,1)} copy(bf16[168,4096]{1,0:T(8,128)(2,1)} %fusion.10) | data formatting | bytes 2752512 | tf_op jit(solution)/shard_map/convert_element_type | solution.py:93
  189.6 4.4 %fusion.63 = f32[64,168,64]{1,2,0:T(8,128)} fusion(bf16[64,168,64]{1,2,0:T(8,128)(2,1)} %bitcast.140, bf16[64,64,64]{2,1,0:T(8,128)(2,1)S(1)} %copy-done.7), kind=kOutput, calls=%fused_computation.126 | convolution fusion | flops 88080384 | bytes 4653056 | tf_op jit(solution)/shard_map/epb,eab->epa/dot_general | solution.py:96
  196.7 26.9 %scatter_fusion = f32[4096,168]{1,0:T(8,128)} fusion(f32[4096,168]{1,0:T(8,128)} %bitcast.131, s32[4096]{0:T(1024)S(1)} %broadcast_select_fusion, f32[4096,168]{1,0:T(8,128)} %bitcast.135), kind=kCustom, calls=%fused_computation.9 | custom fusion | flops 688128 | bytes 8273920
  228.6 15.6 %scatter_fusion.1 = f32[4096,168]{1,0:T(8,128)} fusion(f32[4096,168]{1,0:T(8,128)} %scatter_fusion, s32[2048]{0:T(1024)S(1)} %copy-done.23, f32[2048,168]{1,0:T(8,128)S(1)} %bitcast.138), kind=kCustom, calls=%fused_computation.10 | custom fusion | flops 344064 | bytes 4136960
  244.2 3.7 %convert_element_type.79 = bf16[4096,168]{1,0:T(8,128)(2,1)} convert(f32[4096,168]{1,0:T(8,128)} %scatter_fusion.1) | non-fusion elementwise | flops 688128 | bytes 4128768 | tf_op jit(solution)/shard_map/convert_element_type | solution.py:158
  248.0 4.0 %copy.256 = bf16[64,168,64]{2,0,1:T(8,128)(2,1)S(1)} copy(bf16[64,168,64]{1,2,0:T(8,128)(2,1)} %bitcast.139) | data formatting | bytes 2752512 | tf_op jit(solution)/shard_map/convert_element_type | solution.py:158
  255.1 38.1 %all_to_all.88 = bf16[4,2,86016]{2,1,0:T(2,128)(2,1)} all-to-all(bf16[4,2,86016]{2,1,0:T(2,128)(2,1)} %reshape.560), channel_id=1, replica_groups=mesh['space'=8,'chaos'=4] {'chaos'}, dimensions={0} | all-to-all | bytes 2752512 | tf_op jit(solution)/shard_map/all_to_all | solution.py:159
  293.1 3.5 %reshape.561 = bf16[168,64,64]{2,1,0:T(8,128)(2,1)S(1)} reshape(bf16[4,2,86016]{2,1,0:T(2,128)(2,1)} %all_to_all.88) | data formatting | bytes 2752512
  300.1 5.0 %all_to_all.80 = bf16[256,42,64]{0,2,1:T(8,128)(2,1)} reshape(bf16[4,64,42,64]{1,0,3,2:T(4,128)(2,1)} %copy.257) | data formatting | bytes 2752512 | tf_op jit(solution)/shard_map/all_to_all | solution.py:159
  (185 shorter events, 102.7 us)
Async XLA Ops:
  0.0 49.7 %copy-start = (s32[64]{0:T(128)S(1)}, s32[64]{0:T(128)}, u32[]{:S(2)}) copy-start(s32[64]{0:T(128)} %param.34) | copy-start | bytes 772
  2.4 37.3 %copy-start.32 = (s32[128]{0:T(128)}, s32[128]{0:T(128)S(1)}, u32[]{:S(2)}) copy-start(s32[128]{0:T(128)S(1)} %compare_select_fusion.7) | copy-start | bytes 1540
  4.2 16.0 %all-to-all-start.1 = ((s32[32,8,1]{1,2,0:T(1,128)}), s32[32,8,1]{1,2,0:T(1,128)S(1)}, u32[]{:S(2)}, u32[]{:S(2)}) async-start(s32[32,8,1]{1,2,0:T(1,128)} %bitcast.14), calls=%async_computation.1 | async-start | bytes 32768 | tf_op jit(solution)/shard_map/all_to_all | solution.py:128
  18.2 7.0 %copy-start.30 = (f32[9,64]{1,0:T(8,128)S(1)}, f32[9,64]{1,0:T(8,128)}, u32[]{:S(2)}) copy-start(f32[9,64]{1,0:T(8,128)} %param.21) | copy-start | bytes 6916
  18.2 7.2 %copy-start.22 = (bf16[128,256]{1,0:T(8,128)(2,1)S(1)}, bf16[128,256]{1,0:T(8,128)(2,1)}, u32[]{:S(2)}) copy-start(bf16[128,256]{1,0:T(8,128)(2,1)} %param.30) | copy-start | bytes 196612
  18.2 8.6 %copy-start.29 = (bf16[128,9]{0,1:T(8,128)(2,1)S(1)}, bf16[128,9]{0,1:T(8,128)(2,1)}, u32[]{:S(2)}) copy-start(bf16[128,9]{0,1:T(8,128)(2,1)} %param.32) | copy-start | bytes 6916
  20.2 17.4 %copy-start.10 = (bf16[64,4096]{1,0:T(8,128)(2,1)S(1)}, bf16[64,4096]{1,0:T(8,128)(2,1)}, u32[]{:S(2)}) copy-start(bf16[64,4096]{1,0:T(8,128)(2,1)} %param.20) | copy-start | bytes 1572868
  20.2 19.6 %copy-start.31 = (s32[2]{0:T(128)S(1)}, s32[2]{0:T(128)}, u32[]{:S(2)}) copy-start(s32[2]{0:T(128)} %constant.6) | copy-start | bytes 28
  20.2 20.3 %copy-start.25 = (s32[2688]{0:T(1024)S(1)}, s32[2688]{0:T(1024)}, u32[]{:S(2)}) copy-start(s32[2688]{0:T(1024)} %param.23) | copy-start | bytes 32260
  20.2 20.3 %copy-start.26 = (s32[2688]{0:T(1024)S(1)}, s32[2688]{0:T(1024)}, u32[]{:S(2)}) copy-start(s32[2688]{0:T(1024)} %param.22) | copy-start | bytes 32260
  20.2 20.3 %copy-start.33 = (f32[2688]{0:T(1024)S(1)}, f32[2688]{0:T(1024)}, u32[]{:S(2)}) copy-start(f32[2688]{0:T(1024)} %param.25) | copy-start | bytes 32260
  20.2 20.3 %copy-start.34 = (s32[2688]{0:T(1024)S(1)}, s32[2688]{0:T(1024)}, u32[]{:S(2)}) copy-start(s32[2688]{0:T(1024)} %param.24) | copy-start | bytes 32260
  20.2 42.3 %all-to-all-start = ((bf16[42,4,4096]{2,0,1:T(8,128)(2,1)}), bf16[42,4,4096]{2,0,1:T(8,128)(2,1)S(1)}, u32[]{:S(2)}, u32[]{:S(2)}) async-start(bf16[42,4,4096]{2,0,1:T(8,128)(2,1)} %copy.224), calls=%async_computation | async-start | bytes 3145728 | tf_op jit(solution)/shard_map/all_to_all | solution.py:83
  40.5 11.0 %copy-start.2 = (s32[64]{0:T(128)S(1)}, s32[64]{0:T(128)}, u32[]{:S(2)}) copy-start(s32[64]{0:T(128)} %param.33) | copy-start | bytes 772
  40.5 12.9 %copy-start.24 = (s32[6,16]{1,0:T(8,128)S(1)}, s32[6,16]{1,0:T(8,128)}, u32[]{:S(2)}) copy-start(s32[6,16]{1,0:T(8,128)} %constant.17.clone) | copy-start | bytes 1156
  53.6 13.3 %copy-start.12 = (s32[256,16]{0,1:T(8,128)}, s32[256,16]{0,1:T(8,128)S(1)}, u32[]{:S(2)}) copy-start(s32[256,16]{0,1:T(8,128)S(1)} %multiply_reduce_fusion) | copy-start | bytes 49156
  62.5 15.7 %all-to-all-start.3 = ((bf16[32,8,9]{2,1,0:T(8,128)(2,1)}), bf16[32,8,9]{2,1,0:T(8,128)(2,1)S(1)}, u32[]{:S(2)}, u32[]{:S(2)}) async-start(bf16[32,8,9]{2,1,0:T(8,128)(2,1)} %bitcast.17), calls=%async_computation.3 | async-start | bytes 131072 | tf_op jit(solution)/shard_map/all_to_all | solution.py:127
  78.2 13.6 %copy-start.11 = (bf16[32,8,9]{2,1,0:T(8,128)(2,1)}, bf16[32,8,9]{2,1,0:T(8,128)(2,1)S(1)}, u32[]{:S(2)}) copy-start(bf16[32,8,9]{2,1,0:T(8,128)(2,1)S(1)} %all-to-all-done.3) | copy-start | bytes 13828
  78.2 17.0 %all-to-all-start.2 = ((bf16[32,8,256]{2,1,0:T(8,128)(2,1)}), bf16[32,8,256]{2,1,0:T(8,128)(2,1)}, u32[]{:S(2)}, u32[]{:S(2)}) async-start(bf16[32,8,256]{2,1,0:T(8,128)(2,1)} %bitcast.146), calls=%async_computation.2 | async-start | bytes 262144 | tf_op jit(solution)/shard_map/all_to_all | solution.py:126
  95.2 46.6 %all-to-all-start.4 = ((bf16[32,8,2688]{2,1,0:T(8,128)(2,1)}), bf16[32,8,2688]{2,1,0:T(8,128)(2,1)}, u32[]{:S(2)}, u32[]{:S(2)}) async-start(bf16[32,8,2688]{2,1,0:T(8,128)(2,1)} %bitcast.142), calls=%async_computation.4 | async-start | bytes 2752512 | tf_op jit(solution)/shard_map/all_to_all | solution.py:125
  133.0 5.1 %copy-start.19 = (f32[4096]{0:T(1024)S(1)}, f32[4096]{0:T(1024)}, u32[]{:S(2)}) copy-start(f32[4096]{0:T(1024)} %broadcast_in_dim.91) | copy-start | bytes 49156
  168.8 10.4 %copy-start.13 = (f32[4096]{0:T(1024)S(1)}, f32[4096]{0:T(1024)}, u32[]{:S(2)}) copy-start(f32[4096]{0:T(1024)} %broadcast_in_dim.97) | copy-start | bytes 49156
  173.2 50.4 %all-to-all-start.5 = ((bf16[32,8,2688]{2,1,0:T(8,128)(2,1)}), bf16[32,8,2688]{2,1,0:T(8,128)(2,1)S(1)}, u32[]{:S(2)}, u32[]{:S(2)}) async-start(bf16[32,8,2688]{2,1,0:T(8,128)(2,1)} %all_to_all.74), calls=%async_computation.5 | async-start | bytes 2752512 | tf_op jit(solution)/shard_map/all_to_all | solution.py:148
  305.1 6.4 %copy-start.1 = (s32[64]{0:T(128)S(1)}, s32[64]{0:T(128)}, u32[]{:S(2)}) copy-start(s32[64]{0:T(128)} %param.34) | copy-start | bytes 772
  (17 other events, 43.3 us)
where the time goes:
time: 318 us; the launch traced here: 312 us
  local copies, waits for them, and re-layouts  130 us (41%)
  other arithmetic  58.5 us (18%)
  matrix products  41.6 us (13%)
  blocking collectives  38.1 us (12%)
  starting transfers between devices  34 us (11%)
  waiting for transfers between devices  8.52 us (3%)
    unnamed x8, other arithmetic  45 us
    all_to_all x1, blocking collectives, local(): lax.all_to_all(result, 'chaos', split_axis=1, concat_axis=0, tiled=True)  38.1 us
    gather x1, local copies, waits for them, and re-layouts, local(): own_face = local_field[:, own_nodes]  17.1 us
    convert_element_type x2, local copies, waits for them, and re-layouts, local(): recv_proj.reshape(slot_total, 16, chaos_width).astype(jnp.float32)  12.8 us
    dot_general x8, matrix products, local(): jnp.dot(coupling[mode_idx], local_field, preferred_element_type=jnp.float32)  9.95 us
    gather x1, local copies, waits for them, and re-layouts, local(): die_face = local_field[:, die_nodes]  9.06 us
    all_to_all x1, waiting for transfers between devices, local(): lax.all_to_all(field, 'chaos', split_axis=1, concat_axis=0, tiled=True)  8.51 us
    all_to_all x2, local copies, waits for them, and re-layouts, local(): lax.all_to_all(result, 'chaos', split_axis=1, concat_axis=0, tiled=True)  8.42 us
  transfers between devices with their start and end apart: 6, of which 1 were waited for; matrix products, arithmetic and copies ran while one was open for 45% of the time, Pallas kernels for 0%

commit v1 on v0

v1 whole, which is shorter than its diff:
```python
import functools

import jax
import jax.numpy as jnp
import numpy as np
from jax import lax
from jax.experimental import pallas as pl
from jax.experimental.pallas import tpu as pltpu
from jax.sharding import PartitionSpec as P

ELEM_NODES = 64
LANES = 128
FACE = 16
VMEM_LIMIT = 56 * 1024 * 1024
NT = (((1,), (1,)), ((), ()))
NN = (((1,), (0,)), ((), ()))


def face_nodes():
    node_rows = []
    for side_idx in range(6):
        normal_axis = side_idx // 2
        plane_level = 3 * (side_idx % 2)
        row_nodes = []
        for first_coord in range(4):
            for second_coord in range(4):
                position = [first_coord, second_coord]
                position.insert(normal_axis, plane_level)
                row_nodes.append(16 * position[0] + 4 * position[1] + position[2])
        node_rows.append(row_nodes)
    return np.array(node_rows, dtype=np.int32)


def side_nodes(side_ids):
    node_table = jnp.asarray(face_nodes())
    side_hot = (side_ids[:, None] == jnp.arange(6, dtype=jnp.int32)[None, :]).astype(jnp.int32)
    return jnp.sum(side_hot[:, :, None] * node_table[None, :, :], axis=1)


def mm(a, b, dims=NN):
    return lax.dot_general(a, b, dims, preferred_element_type=jnp.float32)


def iota(shape, dim):
    return lax.broadcasted_iota(jnp.int32, shape, dim)


def hot(mask):
    return jnp.where(mask, 1.0, 0.0).astype(jnp.bfloat16)


def perm_hot(shape, chaos_dim, wide_dim, part, padded):
    i = iota(shape, chaos_dim)
    return hot(iota(shape, wide_dim) == i // part * padded + i % part)


def block_diag(flat):
    spread = mm(hot(iota((LANES, 8), 0) // FACE == iota((LANES, 8), 1)), flat)
    own_row = iota((LANES, 256), 1) // FACE == iota((LANES, 256), 0) % FACE
    spread = jnp.where(own_row, spread, 0.0).astype(jnp.bfloat16)
    fold = hot(iota((256, LANES), 0) % FACE == iota((256, LANES), 1) % FACE)
    tiled = mm(spread, fold)
    same = iota((LANES, LANES), 0) // FACE == iota((LANES, LANES), 1) // FACE
    return jnp.where(same, tiled, 0.0).astype(jnp.bfloat16)


def node_hot(target_row):
    return hot(iota((8 * LANES, LANES), 0) == target_row)


def faces_of(fp_ref, pair_ref, target_ref, group):
    blocks = jnp.concatenate([fp_ref[pair_ref[group * 8 + j]] for j in range(8)], axis=1)
    return mm(blocks, node_hot(target_ref[group])).astype(jnp.bfloat16)


def pack_kernel(owner_col_ref, owner_row_ref, die_ref, int_ref, small_ref, die_out, meta_out, small_out, *, cap):
    segs = owner_row_ref.shape[1]
    slots = die_out.shape[0]
    same = owner_col_ref[...] == owner_row_ref[...]
    before = iota((segs, segs), 0) < iota((segs, segs), 1)
    rank = jnp.sum(jnp.where(same & before, 1.0, 0.0), axis=0, keepdims=True).astype(jnp.int32)
    place = hot(iota((slots, segs), 0) == owner_row_ref[...] * cap + rank)
    die_out[...] = mm(place, die_ref[...]).astype(jnp.bfloat16)
    small = mm(place, small_ref[...])
    small_out[...] = small
    meta_out[:, :256] = mm(place, int_ref[...]).astype(jnp.bfloat16)
    meta_out[:, 256:] = small.astype(jnp.bfloat16)


def project_kernel(pair_ref, f_ref, die_ref, target_ref, fp_out, proj_out, *, part, padded):
    chaos, wide = fp_out.shape[1], f_ref.shape[0]
    perm = perm_hot((chaos, wide), 0, 1, part, padded)
    for p in range(fp_out.shape[0]):
        fp_out[p] = mm(perm, f_ref[:, p * LANES:(p + 1) * LANES]).astype(jnp.bfloat16)

    def step(g, carry):
        face = faces_of(fp_out, pair_ref, target_ref, g)
        mats = block_diag(die_ref[pl.ds(pl.multiple_of(g * 8, 8), 8), :].astype(jnp.bfloat16))
        proj_out[g] = mm(face, mats, NT).astype(jnp.bfloat16)
        return carry

    lax.fori_loop(0, proj_out.shape[0], step, 0, unroll=2)


def mix(coupling_ref, block, weights):
    total = weights[0:1] * block.astype(jnp.float32)
    for k in range(coupling_ref.shape[0]):
        total = total + weights[k + 1:k + 2] * mm(coupling_ref[k], block)
    return total.astype(jnp.bfloat16)


def element_kernel(pair_ref, fp_ref, coupling_ref, kl_ref, stiff_ref, int_ref, target_ref, out_ref, own_out):
    def step(p, carry):
        block = jnp.concatenate([fp_ref[2 * p], fp_ref[2 * p + 1]], axis=1)
        mixed = mix(coupling_ref, block, kl_ref[p])
        out_ref[2 * p] = mm(mixed[:, :LANES], stiff_ref[2 * p], NT)
        out_ref[2 * p + 1] = mm(mixed[:, LANES:], stiff_ref[2 * p + 1], NT)
        return carry

    lax.fori_loop(0, fp_ref.shape[0] // 2, step, 0)

    def own_step(g, carry):
        face = faces_of(fp_ref, pair_ref, target_ref, g)
        mats = block_diag(int_ref[pl.ds(pl.multiple_of(g * 8, 8), 8), :].astype(jnp.bfloat16))
        own_out[g] = mm(face, mats, NT)
        return carry

    lax.fori_loop(0, own_out.shape[0], own_step, 0, unroll=2)


def flux_kernel(recv_ref, own_ref, coupling_ref, coef_ref, flux_out):
    def step(p, carry):
        jump = [
            (recv_ref[2 * p + h].astype(jnp.float32) - own_ref[2 * p + h]).astype(jnp.bfloat16)
            for h in range(2)
        ]
        flux = mix(coupling_ref, jnp.concatenate(jump, axis=1), coef_ref[p])
        flux_out[2 * p] = flux[:, :LANES]
        flux_out[2 * p + 1] = flux[:, LANES:]
        return carry

    lax.fori_loop(0, recv_ref.shape[0] // 2, step, 0)


def scatter_step(pair_ref, flux_ref, mort_ref, target_ref, acc_ref, g, sign):
    mats = block_diag(mort_ref[pl.ds(pl.multiple_of(g * 8, 8), 8), :].astype(jnp.bfloat16))
    spread = mm(mats, node_hot(target_ref[g]), NT).astype(jnp.bfloat16)
    back = mm(flux_ref[g], spread)
    for j in range(8):
        pair = pair_ref[g * 8 + j]
        acc_ref[pair] = acc_ref[pair] + sign * back[:, j * LANES:(j + 1) * LANES]


def own_back_kernel(pair_ref, flux_ref, int_ref, target_ref, start_ref, acc_out):
    acc_out[...] = start_ref[...]

    def step(g, carry):
        scatter_step(pair_ref, flux_ref, int_ref, target_ref, acc_out, g, -1.0)
        return carry

    lax.fori_loop(0, flux_ref.shape[0], step, 0, unroll=2)


def die_back_kernel(pair_ref, flux_ref, die_ref, target_ref, start_ref, out_ref, acc_ref, *, part, padded):
    acc_ref[...] = start_ref[...]

    def step(g, carry):
        scatter_step(pair_ref, flux_ref, die_ref, target_ref, acc_ref, g, 1.0)
        return carry

    lax.fori_loop(0, flux_ref.shape[0], step, 0, unroll=2)
    chaos, wide = acc_ref.shape[1], out_ref.shape[0]
    perm = perm_hot((wide, chaos), 1, 0, part, padded)
    for p in range(acc_ref.shape[0]):
        block = mm(perm, acc_ref[p].astype(jnp.bfloat16)).astype(jnp.bfloat16)
        out_ref[:, p * LANES:(p + 1) * LANES] = block


def call(kernel, outs, args, scalars=0, scratch=()):
    spaces = [pltpu.SMEM] * scalars + [pltpu.VMEM] * (len(args) - scalars)
    return pl.pallas_call(
        kernel,
        out_shape=outs,
        in_specs=[pl.BlockSpec(memory_space=s) for s in spaces],
        out_specs=jax.tree.map(lambda _: pl.BlockSpec(memory_space=pltpu.VMEM), outs),
        scratch_shapes=scratch,
        compiler_params=pltpu.CompilerParams(vmem_limit_bytes=VMEM_LIMIT),
    )(*args)


def dense_coupling(triple_mode, triple_row, triple_col, triple_value, mode_count, chaos_width):
    flat_index = triple_mode * chaos_width + triple_row
    left_hot = (
        flat_index[:, None] == jnp.arange(mode_count * chaos_width, dtype=jnp.int32)[None, :]
    ).astype(jnp.float32)
    right_hot = (triple_col[:, None] == jnp.arange(chaos_width, dtype=jnp.int32)[None, :]).astype(
        jnp.float32
    ) * triple_value[:, None]
    summed = jnp.einsum(
        "ta,tb->ab",
        left_hot,
        right_hot,
        precision=lax.Precision.HIGHEST,
        preferred_element_type=jnp.float32,
    )
    return summed.reshape(mode_count, chaos_width, chaos_width).astype(jnp.bfloat16)


def slot_targets(elem, side):
    slots = elem.shape[0]
    lane_block = (jnp.arange(slots, dtype=jnp.int32) % 8) * LANES + (elem % 2) * ELEM_NODES
    target = lane_block[:, None] + side_nodes(side)
    return elem // 2, target.reshape(slots // 8, 1, LANES)


def lane_weights(rows, repeat):
    rows = jnp.pad(rows, ((0, 16 - rows.shape[0]), (0, 0)))
    per = 256 // repeat
    tiles = rows.shape[1] // per
    rows = jnp.transpose(rows.reshape(16, tiles, per), (1, 0, 2))
    spread = (jnp.arange(per)[:, None] == jnp.arange(256)[None, :] // repeat).astype(jnp.float32)
    return jnp.einsum("tkp,pl->tkl", rows, spread, precision=lax.Precision.HIGHEST)


def local(
    field,
    stiffness,
    kl_coef,
    triple_mode,
    triple_row,
    triple_col,
    triple_value,
    die_elem,
    die_side,
    seg_owner,
    seg_face,
    die_mortar,
    int_mortar,
    bump_coef,
    int_elem,
    int_side,
):
    n_chaos = lax.axis_size("chaos")
    devices = lax.axis_size("space") * n_chaos
    part, local_nodes = field.shape
    chaos = part * n_chaos
    nodes = local_nodes // n_chaos
    padded = -(-part // 16) * 16
    segs = die_elem.shape[0]
    cap = max(2, 2 * segs // devices)
    slots = devices * cap
    groups = slots // 8
    pairs = nodes // LANES
    modes = bump_coef.shape[1] - 1
    bf16, f32 = jnp.bfloat16, jnp.float32
    axes = ("space", "chaos")

    sent = jnp.pad(field, ((0, padded - part), (0, 0))).reshape(padded, n_chaos, nodes)
    sent = jnp.transpose(sent, (1, 0, 2))
    wide = lax.all_to_all(sent, "chaos", split_axis=0, concat_axis=0, tiled=True)
    wide = wide.reshape(n_chaos * padded, nodes)

    ints = jnp.stack([seg_face, die_elem, die_side], axis=1).astype(bf16)
    small = jnp.pad(jnp.concatenate([bump_coef, ints], axis=1), ((0, 0), (0, LANES - modes - 4)))
    die_slots, meta, small_slots = call(
        functools.partial(pack_kernel, cap=cap),
        (
            jax.ShapeDtypeStruct((slots, 256), bf16),
            jax.ShapeDtypeStruct((slots, 256 + LANES), bf16),
            jax.ShapeDtypeStruct((slots, LANES), f32),
        ),
        (seg_owner[:, None], seg_owner[None, :], die_mortar, int_mortar, small),
    )
    meta = lax.all_to_all(meta, axes, split_axis=0, concat_axis=0, tiled=True)
    die_ids = small_slots[:, modes + 2:modes + 4].astype(jnp.int32)
    die_pair, die_target = slot_targets(die_ids[:, 0], die_ids[:, 1])

    coupling = dense_coupling(triple_mode, triple_row, triple_col, triple_value, modes, chaos)
    kl_lanes = lane_weights(kl_coef, ELEM_NODES)
    blocks = stiffness.reshape(pairs, 2, ELEM_NODES, 1, ELEM_NODES)
    on_diag = jnp.eye(2, dtype=bool)[None, :, None, :, None]
    stiff = jnp.where(on_diag, blocks, jnp.zeros((), bf16)).reshape(pairs, LANES, LANES)

    fp, proj = call(
        functools.partial(project_kernel, part=part, padded=padded),
        (
            jax.ShapeDtypeStruct((pairs, chaos, LANES), bf16),
            jax.ShapeDtypeStruct((groups, chaos, LANES), bf16),
        ),
        (die_pair, wide, die_slots, die_target),
        1,
    )

    def exchange(values):
        per = devices // groups
        values = values.reshape(groups, chaos, per, LANES // per)
        values = jnp.transpose(values, (0, 2, 1, 3)).reshape(devices, chaos, LANES // per)
        values = lax.all_to_all(values, axes, split_axis=0, concat_axis=0, tiled=True)
        values = values.reshape(groups, per, chaos, LANES // per)
        return jnp.transpose(values, (0, 2, 1, 3)).reshape(groups, chaos, LANES)

    recv = exchange(proj)

    int_slots = meta[:, :256]
    recv_small = meta[:, 256:256 + modes + 2].astype(f32)
    coef_lanes = lane_weights(recv_small[:, :modes + 1].T, FACE)
    face_hot = recv_small[:, modes + 1].astype(jnp.int32)[:, None] == jnp.arange(int_elem.shape[0])[None, :]
    own_elem = jnp.sum(jnp.where(face_hot, int_elem[None, :], 0), axis=1)
    own_side = jnp.sum(jnp.where(face_hot, int_side[None, :], 0), axis=1)
    own_pair, own_target = slot_targets(own_elem, own_side)

    local_out, own_proj = call(
        element_kernel,
        (
            jax.ShapeDtypeStruct((pairs, chaos, LANES), f32),
            jax.ShapeDtypeStruct((groups, chaos, LANES), f32),
        ),
        (own_pair, fp, coupling, kl_lanes, stiff, int_slots, own_target),
        1,
    )
    flux = call(
        flux_kernel,
        jax.ShapeDtypeStruct((groups, chaos, LANES), bf16),
        (recv, own_proj, coupling, coef_lanes),
    )
    back_flux = exchange(flux)
    local_out = call(
        own_back_kernel,
        jax.ShapeDtypeStruct((pairs, chaos, LANES), f32),
        (own_pair, flux, int_slots, own_target, local_out),
        1,
    )
    result = call(
        functools.partial(die_back_kernel, part=part, padded=padded),
        jax.ShapeDtypeStruct((n_chaos * padded, nodes), bf16),
        (die_pair, back_flux, die_slots, die_target, local_out),
        1,
        (pltpu.VMEM((pairs, chaos, LANES), f32),),
    )
    result = result.reshape(n_chaos, padded, nodes)
    returned = lax.all_to_all(result, "chaos", split_axis=0, concat_axis=0, tiled=True)
    return jnp.transpose(returned[:, :part], (1, 0, 2)).reshape(part, local_nodes)


def solution(mesh):
    in_specs = (
        P("chaos", "space"),
        P(("space", "chaos"), None),
        P(None, ("space", "chaos")),
        P(),
        P(),
        P(),
        P(),
        P(("space", "chaos")),
        P(("space", "chaos")),
        P(("space", "chaos")),
        P(("space", "chaos")),
        P(("space", "chaos"), None),
        P(("space", "chaos"), None),
        P(("space", "chaos"), None),
        P(("space", "chaos")),
        P(("space", "chaos")),
    )
    out_specs = P("chaos", "space")
    return jax.shard_map(local, mesh=mesh, in_specs=in_specs, out_specs=out_specs, check_vma=False)
```

time: 318 us -> 252 us (0.79); the launches traced: 312 us -> 251 us
  local copies, waits for them, and re-layouts: 130 us -> 23.5 us
  Pallas kernels: 0 us -> 99.3 us
  other arithmetic: 58.5 us -> 7.49 us
  waiting for transfers between devices: 8.52 us -> 49.7 us
  matrix products: 41.6 us -> 8.93 us
  starting transfers between devices: 34 us -> 19.7 us
  blocking collectives: 38.1 us -> 42.6 us
    pallas_call x0 -> x6, Pallas kernels: none -> 99.3 us  [call(): pl.pallas_call(kernel, out_shape=outs, in_specs=[pl.BlockSpec(memory_spac...]
    unnamed x8 -> x0, other arithmetic: 45 us -> none
    all_to_all x6 -> x4, waiting for transfers between devices: 8.52 us -> 49.7 us  [the longest x1 34.2 us: local(): lax.all_to_all(sent, 'chaos', split_axis=0, concat_axis=0, tiled=True)]
    dot_general x21 -> x2, matrix products: 33.9 us -> 2.03 us  [lane_weights(): jnp.einsum('tkp,pl->tkl', rows, spread, precision=lax.Precision.HIGHEST)]
    gather x6 -> x0, local copies, waits for them, and re-layouts: 31.3 us -> none  [the longest x1 17.1 us: local(): own_face = local_field[:, own_nodes]]
    convert_element_type x8 -> x1, local copies, waits for them, and re-layouts: 28.2 us -> 1.18 us  [dense_coupling(): summed.reshape(mode_count, chaos_width, chaos_width).astype(jnp.bfloat16)]
    all_to_all x11 -> x0, local copies, waits for them, and re-layouts: 22.8 us -> none  [the longest x2 8.42 us: local(): lax.all_to_all(result, 'chaos', split_axis=1, concat_axis=0, tiled=True)]
    all_to_all x6 -> x4, starting transfers between devices: 34 us -> 19.7 us  [the longest x2 8.66 us: exchange(): lax.all_to_all(values, axes, split_axis=0, concat_axis=0, tiled=True)]
  transfers between devices with their start and end apart: 6 -> 4, of which waited for: 1 -> 3; matrix products, arithmetic and copies ran while one was open for 45% -> 11% of each run, Pallas kernels for 0% -> 19%
where the time goes in v1:
time: 252 us; the launch traced here: 251 us
  Pallas kernels  99.3 us (39%)
  waiting for transfers between devices  49.7 us (20%)
  blocking collectives  42.6 us (17%)
  local copies, waits for them, and re-layouts  23.5 us (9%)
  starting transfers between devices  19.7 us (8%)
  matrix products  8.93 us (4%)
  other arithmetic  7.49 us (3%)
    pallas_call x6, Pallas kernels, call(): pl.pallas_call(kernel, out_shape=outs, in_specs=[pl.BlockSpec(memory_spac...  99.3 us
    all_to_all x1, blocking collectives, local(): lax.all_to_all(result, 'chaos', split_axis=0, concat_axis=0, tiled=True)  42.6 us
    all_to_all x1, waiting for transfers between devices, local(): lax.all_to_all(sent, 'chaos', split_axis=0, concat_axis=0, tiled=True)  34.2 us
    all_to_all x2, waiting for transfers between devices, exchange(): lax.all_to_all(values, axes, split_axis=0, concat_axis=0, tiled=True)  8.92 us
    all_to_all x2, starting transfers between devices, exchange(): lax.all_to_all(values, axes, split_axis=0, concat_axis=0, tiled=True)  8.66 us
    broadcast_in_dim x5, local copies, waits for them, and re-layouts, local(): jnp.where(on_diag, blocks, jnp.zeros((), bf16)).reshape(pairs, LANES, LANES)  7.36 us
    all_to_all x1, starting transfers between devices, local(): meta = lax.all_to_all(meta, axes, split_axis=0, concat_axis=0, tiled=True)  7.3 us
    unnamed x37, local copies, waits for them, and re-layouts  7.17 us
  transfers between devices with their start and end apart: 4, of which 3 were waited for; matrix products, arithmetic and copies ran while one was open for 11% of the time, Pallas kernels for 19%

profile of v1, /device:TPU:0, one launch (start us, length us, event | category | flops | bytes accessed | tf_op | source)
XLA Modules:
  0.0 251.4 jit_solution(9297502963985375584)
XLA Ops:
  0.0 1.4 copy.74.owner_col_ref
  4.2 2.0 shard_map.172
  6.2 7.3 %all-to-all-start.2 = ((bf16[32,8,384]{2,1,0:T(8,128)(2,1)}), bf16[32,8,384]{2,1,0:T(8,128)(2,1)S(1)}, u32[]{:S(2)}, u32[]{:S(2)}) async-start(bf16[32,8,384]{2,1,0:T(8,128)(2,1)} %bitcast.58), calls=%async_computation.2 | async-start | bytes 393216 | tf_op jit(solution)/shard_map/all_to_all | solution.py:274
  13.5 1.5 pad.17
  15.0 1.2 copy.96
  16.2 6.6 %all-to-all-done.2 = bf16[32,8,384]{2,1,0:T(8,128)(2,1)S(1)} async-done(((bf16[32,8,384]{2,1,0:T(8,128)(2,1)}), bf16[32,8,384]{2,1,0:T(8,128)(2,1)S(1)}, u32[]{:S(2)}, u32[]{:S(2)}) %all-to-all-start.2) | async-done | bytes 196640 | tf_op jit(solution)/shard_map/all_to_all | solution.py:274
  22.8 3.7 %all-to-all-start = ((bf16[4,48,4096]{2,1,0:T(8,128)(2,1)}), bf16[4,48,4096]{2,1,0:T(8,128)(2,1)S(1)}, u32[]{:S(2)}, u32[]{:S(2)}) async-start(bf16[4,48,4096]{2,1,0:T(8,128)(2,1)} %bitcast.46), calls=%async_computation | async-start | bytes 3145728 | tf_op jit(solution)/shard_map/all_to_all | solution.py:260
  29.7 34.2 %all-to-all-done = bf16[4,48,4096]{2,1,0:T(8,128)(2,1)S(1)} async-done(((bf16[4,48,4096]{2,1,0:T(8,128)(2,1)}), bf16[4,48,4096]{2,1,0:T(8,128)(2,1)S(1)}, u32[]{:S(2)}, u32[]{:S(2)}) %all-to-all-start) | async-done | bytes 1572896 | tf_op jit(solution)/shard_map/all_to_all | solution.py:260
  65.0 16.8 %shard_map.173 = (bf16[32,168,128]{2,1,0:T(8,128)(2,1)}, bf16[32,168,128]{2,1,0:T(8,128)(2,1)}) custom-call(s32[256]{0:T(256)} %and_select_fusion.3.pair_ref, bf16[192,4096]{1,0:T(8,128)(2,1)} %bitcast.47, bf16[256,256]{1,0:T(8,128)(2,1)} %get-tuple-element.13.die_ref, s32[32,1,128]{2,1,0:T(1,128)} %bitcast.59), custom_call_target="tpu_custom_call" | custom-call | tf_op jit(solution)/shard_map/pallas_call | solution.py:181
  81.8 3.0 %all-to-all-start.1 = ((bf16[32,168,128]{2,1,0:T(8,128)(2,1)}), bf16[32,168,128]{2,1,0:T(8,128)(2,1)S(1)}, u32[]{:S(2)}, u32[]{:S(2)}) async-start(bf16[32,168,128]{2,1,0:T(8,128)(2,1)} %get-tuple-element.14), calls=%async_computation.1 | async-start | bytes 2752512 | tf_op jit(solution)/shard_map/all_to_all | solution.py:298
  84.9 6.9 %fusion.3 = bf16[1344,168]{0,1:T(8,128)(2,1)S(1)} fusion(s32[2688]{0:T(1024)S(1)} %multiply_add_fusion, f32[2688]{0:T(1024)S(1)} %copy-done.15, s32[2688]{0:T(1024)S(1)} %copy-done.16), kind=kOutput, calls=%fused_computation.5 | convolution fusion | flops 7287888384 | bytes 483840 | tf_op jit(solution)/shard_map/ta,tb->ab/dot_general | solution.py:199
  91.8 1.2 copy.80
  93.1 2.1 broadcast_in_dim.82
  95.2 3.3 %broadcast_in_dim.83 = bf16[32,2,64,2,64]{4,3,2,1,0:T(2,128)(2,1)S(1)} broadcast(bf16[32,2,64,64]{3,2,1,0:T(8,128)(2,1)} %broadcast_in_dim.82), dimensions={0,1,2,4} | broadcast | bytes 1572864 | tf_op jit(solution)/shard_map/jit(_where)/broadcast_in_dim | solution.py:282
  98.5 1.8 broadcast_in_dim.84
  101.6 2.3 broadcast_select_fusion.stiff_ref
  107.3 24.8 %shard_map.174 = (f32[32,168,128]{2,1,0:T(8,128)}, f32[32,168,128]{2,1,0:T(8,128)}) custom-call(s32[256]{0:T(256)} %and_select_fusion.2.pair_ref, bf16[32,168,128]{2,1,0:T(8,128)(2,1)} %get-tuple-element.16.fp_ref, bf16[8,168,168]{2,1,0:T(8,128)(2,1)} %bitcast.51, f32[16,16,256]{2,1,0:T(8,128)} %fusion.33.kl_ref, ...), custom_call_target="tpu_custom_call" | custom-call | tf_op jit(solution)/shard_map/pallas_call | solution.py:181
  133.2 9.2 %shard_map.175.flux_ref = bf16[32,168,128]{2,1,0:T(8,128)(2,1)} custom-call(bf16[32,168,128]{2,1,0:T(8,128)(2,1)} %copy-done.1, f32[32,168,128]{2,1,0:T(8,128)} %get-tuple-element.17.own_ref, bf16[8,168,168]{2,1,0:T(8,128)(2,1)} %bitcast.52, f32[16,16,256]{2,1,0:T(8,128)} %fusion.15.coef_ref), custom_call_target="tpu_custom_call" | custom-call | tf_op jit(solution)/shard_map/pallas_call | solution.py:181
  142.4 5.7 %all-to-all-start.3 = ((bf16[32,168,128]{2,1,0:T(8,128)(2,1)}), bf16[32,168,128]{2,1,0:T(8,128)(2,1)S(1)}, u32[]{:S(2)}, u32[]{:S(2)}) async-start(bf16[32,168,128]{2,1,0:T(8,128)(2,1)} %shard_map.175.flux_ref), calls=%async_computation.3 | async-start | bytes 2752512 | tf_op jit(solution)/shard_map/all_to_all | solution.py:298
  148.1 22.9 %shard_map.176.start_ref = f32[32,168,128]{2,1,0:T(8,128)} custom-call(s32[256]{0:T(256)} %and_select_fusion.2.pair_ref, bf16[32,168,128]{2,1,0:T(8,128)(2,1)} %shard_map.175.flux_ref, bf16[256,256]{1,0:T(8,128)(2,1)} %slice.39.int_ref, s32[32,1,128]{2,1,0:T(1,128)} %bitcast.62, f32[32,168,128]{2,1,0:T(8,128)} %get-tuple-element.18.start_ref), custom_call_target="tpu_custom_call" | custom-call | tf_op jit(solution)/shard_map/pallas_call | solution.py:181
  171.0 8.9 %all-to-all-done.3.flux_ref = bf16[32,168,128]{2,1,0:T(8,128)(2,1)S(1)} async-done(((bf16[32,168,128]{2,1,0:T(8,128)(2,1)}), bf16[32,168,128]{2,1,0:T(8,128)(2,1)S(1)}, u32[]{:S(2)}, u32[]{:S(2)}) %all-to-all-start.3) | async-done | bytes 1376288 | tf_op jit(solution)/shard_map/all_to_all | solution.py:298
  181.0 23.6 %shard_map.177 = bf16[192,4096]{1,0:T(8,128)(2,1)} custom-call(s32[256]{0:T(256)} %and_select_fusion.3.pair_ref, bf16[32,168,128]{2,1,0:T(8,128)(2,1)} %copy-done.2, bf16[256,256]{1,0:T(8,128)(2,1)} %get-tuple-element.13.die_ref, s32[32,1,128]{2,1,0:T(1,128)} %bitcast.60, f32[32,168,128]{2,1,0:T(8,128)} %shard_map.176.start_ref), custom_call_target="tpu_custom_call" | custom-call | tf_op jit(solution)/shard_map/pallas_call | solution.py:181
  204.6 42.6 %all_to_all.32 = bf16[4,48,4096]{2,1,0:T(8,128)(2,1)S(1)} all-to-all(bf16[4,48,4096]{2,1,0:T(8,128)(2,1)} %bitcast.49), channel_id=1, replica_groups=mesh['space'=8,'chaos'=4] {'chaos'}, dimensions={0} | all-to-all | bytes 3145728 | tf_op jit(solution)/shard_map/all_to_all | solution.py:341
  249.4 2.0 copy.94
  (82 shorter events, 16.2 us)
Async XLA Ops:
  6.2 16.6 %all-to-all-start.2 = ((bf16[32,8,384]{2,1,0:T(8,128)(2,1)}), bf16[32,8,384]{2,1,0:T(8,128)(2,1)S(1)}, u32[]{:S(2)}, u32[]{:S(2)}) async-start(bf16[32,8,384]{2,1,0:T(8,128)(2,1)} %bitcast.58), calls=%async_computation.2 | async-start | bytes 393216 | tf_op jit(solution)/shard_map/all_to_all | solution.py:274
  22.8 5.0 %copy-start.5 = (bf16[32,8,384]{2,1,0:T(8,128)(2,1)}, bf16[32,8,384]{2,1,0:T(8,128)(2,1)S(1)}, u32[]{:S(2)}) copy-start(bf16[32,8,384]{2,1,0:T(8,128)(2,1)S(1)} %all-to-all-done.2) | copy-start | bytes 589828
  22.8 3.7 %copy-start.8 = (f32[256,128]{1,0:T(8,128)S(1)}, f32[256,128]{1,0:T(8,128)}, u32[]{:S(2)}) copy-start(f32[256,128]{1,0:T(8,128)} %get-tuple-element.12) | copy-start | bytes 393220
  22.8 5.8 %copy-start.13 = (s32[64]{0:T(128)S(1)}, s32[64]{0:T(128)}, u32[]{:S(2)}) copy-start(s32[64]{0:T(128)} %param.33) | copy-start | bytes 772
  22.8 5.8 %copy-start.14 = (s32[64]{0:T(128)S(1)}, s32[64]{0:T(128)}, u32[]{:S(2)}) copy-start(s32[64]{0:T(128)} %param.32) | copy-start | bytes 772
  22.8 6.0 %copy-start.12 = (s32[6,16]{1,0:T(8,128)S(1)}, s32[6,16]{1,0:T(8,128)}, u32[]{:S(2)}) copy-start(s32[6,16]{1,0:T(8,128)} %constant.97.clone) | copy-start | bytes 1156
  22.8 41.0 %all-to-all-start = ((bf16[4,48,4096]{2,1,0:T(8,128)(2,1)}), bf16[4,48,4096]{2,1,0:T(8,128)(2,1)S(1)}, u32[]{:S(2)}, u32[]{:S(2)}) async-start(bf16[4,48,4096]{2,1,0:T(8,128)(2,1)} %bitcast.46), calls=%async_computation | async-start | bytes 3145728 | tf_op jit(solution)/shard_map/all_to_all | solution.py:260
  27.8 0.7 copy-start.3
  63.9 1.1 copy-start
  81.8 3.0 %copy-start.9 = (s32[2688]{0:T(1024)S(1)}, s32[2688]{0:T(1024)}, u32[]{:S(2)}) copy-start(s32[2688]{0:T(1024)} %param.22) | copy-start | bytes 32260
  81.8 3.0 %copy-start.10 = (s32[2688]{0:T(1024)S(1)}, s32[2688]{0:T(1024)}, u32[]{:S(2)}) copy-start(s32[2688]{0:T(1024)} %param.21) | copy-start | bytes 32260
  81.8 3.1 %copy-start.15 = (f32[2688]{0:T(1024)S(1)}, f32[2688]{0:T(1024)}, u32[]{:S(2)}) copy-start(f32[2688]{0:T(1024)} %param.24) | copy-start | bytes 32260
  81.8 3.1 %copy-start.16 = (s32[2688]{0:T(1024)S(1)}, s32[2688]{0:T(1024)}, u32[]{:S(2)}) copy-start(s32[2688]{0:T(1024)} %param.23) | copy-start | bytes 32260
  81.8 50.3 %all-to-all-start.1 = ((bf16[32,168,128]{2,1,0:T(8,128)(2,1)}), bf16[32,168,128]{2,1,0:T(8,128)(2,1)S(1)}, u32[]{:S(2)}, u32[]{:S(2)}) async-start(bf16[32,168,128]{2,1,0:T(8,128)(2,1)} %get-tuple-element.14), calls=%async_computation.1 | async-start | bytes 2752512 | tf_op jit(solution)/shard_map/all_to_all | solution.py:298
  84.9 8.1 %copy-start.11 = (f32[9,64]{1,0:T(8,128)S(1)}, f32[9,64]{1,0:T(8,128)}, u32[]{:S(2)}) copy-start(f32[9,64]{1,0:T(8,128)} %param.20) | copy-start | bytes 6916
  84.9 8.2 %copy-start.7 = (bf16[64,4096]{1,0:T(8,128)(2,1)S(1)}, bf16[64,4096]{1,0:T(8,128)(2,1)}, u32[]{:S(2)}) copy-start(bf16[64,4096]{1,0:T(8,128)(2,1)} %param.19) | copy-start | bytes 1572868
  100.2 3.6 %copy-start.6 = (bf16[32,8,384]{2,1,0:T(8,128)(2,1)S(1)}, bf16[32,8,384]{2,1,0:T(8,128)(2,1)}, u32[]{:S(2)}) copy-start(bf16[32,8,384]{2,1,0:T(8,128)(2,1)} %copy-done.5) | copy-start | bytes 589828
  100.5 4.5 %copy-start.4 = (f32[256,10]{1,0:T(8,128)S(1)}, f32[256,10]{1,0:T(8,128)}, u32[]{:S(2)}) copy-start(f32[256,10]{1,0:T(8,128)} %copy-done.3) | copy-start | bytes 30724
  132.1 1.1 copy-start.1
  142.4 37.5 %all-to-all-start.3 = ((bf16[32,168,128]{2,1,0:T(8,128)(2,1)}), bf16[32,168,128]{2,1,0:T(8,128)(2,1)S(1)}, u32[]{:S(2)}, u32[]{:S(2)}) async-start(bf16[32,168,128]{2,1,0:T(8,128)(2,1)} %shard_map.175.flux_ref), calls=%async_computation.3 | async-start | bytes 2752512 | tf_op jit(solution)/shard_map/all_to_all | solution.py:298
  179.9 1.1 copy-start.2

commit v2 on v1

--- a/solution.py
+++ b/solution.py
@@ -68,9 +68,46 @@
     return hot(iota((8 * LANES, LANES), 0) == target_row)
 
 
-def faces_of(fp_ref, pair_ref, target_ref, group):
-    blocks = jnp.concatenate([fp_ref[pair_ref[group * 8 + j]] for j in range(8)], axis=1)
-    return mm(blocks, node_hot(target_ref[group])).astype(jnp.bfloat16)
+def faces_of(fp_ref, pair_ref, group):
+    return jnp.concatenate([fp_ref[pair_ref[group * 8 + j]] for j in range(8)], axis=1)
+
+
+def weave_kernel(mort_ref, target_ref, out_ref):
+    for h in range(out_ref.shape[0]):
+        mats = block_diag(mort_ref[h])
+        out_ref[h] = mm(mats, node_hot(target_ref[h]), NT).astype(jnp.bfloat16)
+
+
+def tail_hot(shape, dense_dim, low):
+    dense, row = iota(shape, dense_dim), iota(shape, 1 - dense_dim)
+    return hot((row // 16 == dense // low) & (row % 16 == dense % low))
+
+
+def send_kernel(field_ref, out_ref):
+    part, nodes = field_ref.shape
+    high = part // 16 * 16
+    low, width = part - high, nodes // 16
+    total = jnp.zeros((16 * low, width), jnp.float32)
+    for q in range(16):
+        cols = slice(q * width, (q + 1) * width)
+        out_ref[0, q * high:(q + 1) * high, :] = field_ref[:high, cols]
+        shape = (16 * low, low)
+        place = hot(iota(shape, 0) == q * low + iota(shape, 1))
+        total = total + mm(place, field_ref[high:part, cols])
+    out_ref[0, 16 * high:, :] = total.astype(jnp.bfloat16)
+
+
+def receive_kernel(in_ref, out_ref):
+    part, nodes = out_ref.shape
+    high = part // 16 * 16
+    low, width = part - high, nodes // 16
+    tail = in_ref[0, 16 * high:, :]
+    for q in range(16):
+        cols = slice(q * width, (q + 1) * width)
+        out_ref[:high, cols] = in_ref[0, q * high:(q + 1) * high, :]
+        shape = (low, 16 * low)
+        pick = hot(iota(shape, 1) == q * low + iota(shape, 0))
+        out_ref[high:part, cols] = mm(pick, tail).astype(jnp.bfloat16)
 
 
 def pack_kernel(owner_col_ref, owner_row_ref, die_ref, int_ref, small_ref, die_out, meta_out, small_out, *, cap):
@@ -87,19 +124,41 @@
     meta_out[:, 256:] = small.astype(jnp.bfloat16)
 
 
-def project_kernel(pair_ref, f_ref, die_ref, target_ref, fp_out, proj_out, *, part, padded):
-    chaos, wide = fp_out.shape[1], f_ref.shape[0]
-    perm = perm_hot((chaos, wide), 0, 1, part, padded)
-    for p in range(fp_out.shape[0]):
-        fp_out[p] = mm(perm, f_ref[:, p * LANES:(p + 1) * LANES]).astype(jnp.bfloat16)
-
-    def step(g, carry):
-        face = faces_of(fp_out, pair_ref, target_ref, g)
-        mats = block_diag(die_ref[pl.ds(pl.multiple_of(g * 8, 8), 8), :].astype(jnp.bfloat16))
-        proj_out[g] = mm(face, mats, NT).astype(jnp.bfloat16)
-        return carry
-
-    lax.fori_loop(0, proj_out.shape[0], step, 0, unroll=2)
+def unpack(wide_ref, fp_out, part):
+    n_chaos, rows, width = wide_ref.shape
+    high = part // 16 * 16
+    low = part - high
+    padded = high + 16
+    spread = tail_hot((256, 16 * low), 1, low)
+    tails = [mm(spread, wide_ref[c, 16 * high:, :]).astype(jnp.bfloat16) for c in range(n_chaos)]
+    perm = perm_hot((part * n_chaos, padded * n_chaos), 0, 1, part, padded)
+    per = width // LANES
+    for q in range(16):
+        pieces = []
+        for c in range(n_chaos):
+            pieces.append(wide_ref[c, q * high:(q + 1) * high, :])
+            pieces.append(tails[c][q * 16:(q + 1) * 16])
+        block = mm(perm, jnp.concatenate(pieces, axis=0)).astype(jnp.bfloat16)
+        for h in range(per):
+            fp_out[q * per + h] = block[:, h * LANES:(h + 1) * LANES]
+
+
+def project_kernel(pair_ref, wide_ref, weave_ref, fp_out, proj_out, *, part):
+    step = pl.program_id(0)
+
+    @pl.when(step == 0)
+    def _():
+        unpack(wide_ref, fp_out, part)
+
+    for h in range(proj_out.shape[0]):
+        face = faces_of(fp_out, pair_ref, step * proj_out.shape[0] + h)
+        proj_out[h] = mm(face, weave_ref[h], NT).astype(jnp.bfloat16)
+
+
+def own_project_kernel(pair_ref, fp_ref, weave_ref, proj_out):
+    for h in range(proj_out.shape[0]):
+        face = faces_of(fp_ref, pair_ref, pl.program_id(0) * proj_out.shape[0] + h)
+        proj_out[h] = mm(face, weave_ref[h], NT)
 
 
 def mix(coupling_ref, block, weights):
@@ -109,7 +168,7 @@
     return total.astype(jnp.bfloat16)
 
 
-def element_kernel(pair_ref, fp_ref, coupling_ref, kl_ref, stiff_ref, int_ref, target_ref, out_ref, own_out):
+def element_kernel(fp_ref, coupling_ref, kl_ref, stiff_ref, out_ref):
     def step(p, carry):
         block = jnp.concatenate([fp_ref[2 * p], fp_ref[2 * p + 1]], axis=1)
         mixed = mix(coupling_ref, block, kl_ref[p])
@@ -118,14 +177,6 @@
         return carry
 
     lax.fori_loop(0, fp_ref.shape[0] // 2, step, 0)
-
-    def own_step(g, carry):
-        face = faces_of(fp_ref, pair_ref, target_ref, g)
-        mats = block_diag(int_ref[pl.ds(pl.multiple_of(g * 8, 8), 8), :].astype(jnp.bfloat16))
-        own_out[g] = mm(face, mats, NT)
-        return carry
-
-    lax.fori_loop(0, own_out.shape[0], own_step, 0, unroll=2)
 
 
 def flux_kernel(recv_ref, own_ref, coupling_ref, coef_ref, flux_out):
@@ -142,50 +193,77 @@
     lax.fori_loop(0, recv_ref.shape[0] // 2, step, 0)
 
 
-def scatter_step(pair_ref, flux_ref, mort_ref, target_ref, acc_ref, g, sign):
-    mats = block_diag(mort_ref[pl.ds(pl.multiple_of(g * 8, 8), 8), :].astype(jnp.bfloat16))
-    spread = mm(mats, node_hot(target_ref[g]), NT).astype(jnp.bfloat16)
-    back = mm(flux_ref[g], spread)
-    for j in range(8):
-        pair = pair_ref[g * 8 + j]
-        acc_ref[pair] = acc_ref[pair] + sign * back[:, j * LANES:(j + 1) * LANES]
-
-
-def own_back_kernel(pair_ref, flux_ref, int_ref, target_ref, start_ref, acc_out):
-    acc_out[...] = start_ref[...]
-
-    def step(g, carry):
-        scatter_step(pair_ref, flux_ref, int_ref, target_ref, acc_out, g, -1.0)
-        return carry
-
-    lax.fori_loop(0, flux_ref.shape[0], step, 0, unroll=2)
-
-
-def die_back_kernel(pair_ref, flux_ref, die_ref, target_ref, start_ref, out_ref, acc_ref, *, part, padded):
-    acc_ref[...] = start_ref[...]
-
-    def step(g, carry):
-        scatter_step(pair_ref, flux_ref, die_ref, target_ref, acc_ref, g, 1.0)
-        return carry
-
-    lax.fori_loop(0, flux_ref.shape[0], step, 0, unroll=2)
-    chaos, wide = acc_ref.shape[1], out_ref.shape[0]
-    perm = perm_hot((wide, chaos), 1, 0, part, padded)
-    for p in range(acc_ref.shape[0]):
-        block = mm(perm, acc_ref[p].astype(jnp.bfloat16)).astype(jnp.bfloat16)
-        out_ref[:, p * LANES:(p + 1) * LANES] = block
-
-
-def call(kernel, outs, args, scalars=0, scratch=()):
-    spaces = [pltpu.SMEM] * scalars + [pltpu.VMEM] * (len(args) - scalars)
-    return pl.pallas_call(
+def scatter_step(pair_ref, flux_ref, weave_ref, acc_ref, sign):
+    for h in range(flux_ref.shape[0]):
+        back = mm(flux_ref[h], weave_ref[h])
+        for j in range(8):
+            pair = pair_ref[(pl.program_id(0) * flux_ref.shape[0] + h) * 8 + j]
+            acc_ref[pair] = acc_ref[pair] + sign * back[:, j * LANES:(j + 1) * LANES]
+
+
+def own_back_kernel(pair_ref, flux_ref, weave_ref, start_ref, acc_out):
+    @pl.when(pl.program_id(0) == 0)
+    def _():
+        acc_out[...] = start_ref[...]
+
+    scatter_step(pair_ref, flux_ref, weave_ref, acc_out, -1.0)
+
+
+def die_back_kernel(pair_ref, flux_ref, weave_ref, start_ref, out_ref, acc_ref, tail_ref, *, part):
+    @pl.when(pl.program_id(0) == 0)
+    def _():
+        acc_ref[...] = start_ref[...]
+
+    scatter_step(pair_ref, flux_ref, weave_ref, acc_ref, 1.0)
+
+    @pl.when(pl.program_id(0) == pl.num_programs(0) - 1)
+    def _():
+        n_chaos, rows, width = out_ref.shape
+        high = part // 16 * 16
+        low = part - high
+        padded = high + 16
+        perm = perm_hot((padded * n_chaos, part * n_chaos), 1, 0, part, padded)
+        per = width // LANES
+        for q in range(16):
+            block = jnp.concatenate([acc_ref[q * per + h].astype(jnp.bfloat16) for h in range(per)], axis=1)
+            block = mm(perm, block).astype(jnp.bfloat16)
+            for c in range(n_chaos):
+                out_ref[c, q * high:(q + 1) * high, :] = block[c * padded:c * padded + high]
+                tail_ref[c, q * 16:(q + 1) * 16, :] = block[c * padded + high:(c + 1) * padded]
+        gather = tail_hot((16 * low, 256), 0, low)
+        for c in range(n_chaos):
+            out_ref[c, 16 * high:, :] = mm(gather, tail_ref[c]).astype(jnp.bfloat16)
+
+
+def call(kernel, outs, args, scalars=0, scratch=(), steps=0, split=(), split_outs=()):
+    many = isinstance(outs, tuple)
+    shapes = outs if many else (outs,)
+
+    def spec(shape, cut):
+        if steps == 0:
+            return pl.BlockSpec(memory_space=pltpu.VMEM)
+        rest = (0,) * (len(shape) - 1)
+        if cut:
+            return pl.BlockSpec((shape[0] // steps,) + tuple(shape[1:]), lambda i: (i,) + rest)
+        return pl.BlockSpec(tuple(shape), lambda i: (0,) + rest)
+
+    in_specs = [
+        pl.BlockSpec(memory_space=pltpu.SMEM) if n < scalars else spec(x.shape, n in split)
+        for n, x in enumerate(args)
+    ]
+    out_specs = tuple(spec(x.shape, n in split_outs) for n, x in enumerate(shapes))
+    moved = sum(x.size * x.dtype.itemsize for x in (*args, *shapes))
+    result = pl.pallas_call(
         kernel,
-        out_shape=outs,
-        in_specs=[pl.BlockSpec(memory_space=s) for s in spaces],
-        out_specs=jax.tree.map(lambda _: pl.BlockSpec(memory_space=pltpu.VMEM), outs),
+        out_shape=shapes,
+        grid=(steps,) if steps else (),
+        in_specs=in_specs,
+        out_specs=out_specs,
         scratch_shapes=scratch,
         compiler_params=pltpu.CompilerParams(vmem_limit_bytes=VMEM_LIMIT),
+        cost_estimate=pl.CostEstimate(flops=0, bytes_accessed=moved, transcendentals=0),
     )(*args)
+    return result if many else result[0]
 
 
 def dense_coupling(triple_mode, triple_row, triple_col, triple_value, mode_count, chaos_width):
@@ -245,7 +323,6 @@
     part, local_nodes = field.shape
     chaos = part * n_chaos
     nodes = local_nodes // n_chaos
-    padded = -(-part // 16) * 16
     segs = die_elem.shape[0]
     cap = max(2, 2 * segs // devices)
     slots = devices * cap
@@ -255,10 +332,14 @@
     bf16, f32 = jnp.bfloat16, jnp.float32
     axes = ("space", "chaos")
 
-    sent = jnp.pad(field, ((0, padded - part), (0, 0))).reshape(padded, n_chaos, nodes)
-    sent = jnp.transpose(sent, (1, 0, 2))
+    sent = pl.pallas_call(
+        send_kernel,
+        out_shape=jax.ShapeDtypeStruct((n_chaos, 16 * part, nodes // 16), bf16),
+        grid=(n_chaos,),
+        in_specs=[pl.BlockSpec((part, nodes), lambda c: (0, c))],
+        out_specs=pl.BlockSpec((1, 16 * part, nodes // 16), lambda c: (c, 0, 0)),
+    )(field)
     wide = lax.all_to_all(sent, "chaos", split_axis=0, concat_axis=0, tiled=True)
-    wide = wide.reshape(n_chaos * padded, nodes)
 
     ints = jnp.stack([seg_face, die_elem, die_side], axis=1).astype(bf16)
     small = jnp.pad(jnp.concatenate([bump_coef, ints], axis=1), ((0, 0), (0, LANES - modes - 4)))
@@ -271,7 +352,6 @@
         ),
         (seg_owner[:, None], seg_owner[None, :], die_mortar, int_mortar, small),
     )
-    meta = lax.all_to_all(meta, axes, split_axis=0, concat_axis=0, tiled=True)
     die_ids = small_slots[:, modes + 2:modes + 4].astype(jnp.int32)
     die_pair, die_target = slot_targets(die_ids[:, 0], die_ids[:, 1])
 
@@ -281,15 +361,35 @@
     on_diag = jnp.eye(2, dtype=bool)[None, :, None, :, None]
     stiff = jnp.where(on_diag, blocks, jnp.zeros((), bf16)).reshape(pairs, LANES, LANES)
 
+    groups3 = (groups, 8, 256)
+    weave_shape = jax.ShapeDtypeStruct((groups, LANES, 8 * LANES), bf16)
+    steps = groups // 4
+    die_weave = call(
+        weave_kernel,
+        weave_shape,
+        (die_slots.reshape(groups3), die_target),
+        steps=steps,
+        split=(0, 1),
+        split_outs=(0,),
+    )
+    wide, meta, die_weave, die_pair, coupling, kl_lanes, stiff = lax.optimization_barrier(
+        (wide, meta, die_weave, die_pair, coupling, kl_lanes, stiff)
+    )
+    meta = lax.all_to_all(meta, axes, split_axis=0, concat_axis=0, tiled=True)
     fp, proj = call(
-        functools.partial(project_kernel, part=part, padded=padded),
+        functools.partial(project_kernel, part=part),
         (
             jax.ShapeDtypeStruct((pairs, chaos, LANES), bf16),
             jax.ShapeDtypeStruct((groups, chaos, LANES), bf16),
         ),
-        (die_pair, wide, die_slots, die_target),
+        (die_pair, wide, die_weave),
         1,
-    )
+        steps=steps,
+        split=(2,),
+        split_outs=(1,),
+    )
+
+    meta, proj = lax.optimization_barrier((meta, proj))
 
     def exchange(values):
         per = devices // groups
@@ -309,14 +409,27 @@
     own_side = jnp.sum(jnp.where(face_hot, int_side[None, :], 0), axis=1)
     own_pair, own_target = slot_targets(own_elem, own_side)
 
-    local_out, own_proj = call(
+    int_weave = call(
+        weave_kernel,
+        weave_shape,
+        (int_slots.reshape(groups3), own_target),
+        steps=steps,
+        split=(0, 1),
+        split_outs=(0,),
+    )
+    local_out = call(
         element_kernel,
-        (
-            jax.ShapeDtypeStruct((pairs, chaos, LANES), f32),
-            jax.ShapeDtypeStruct((groups, chaos, LANES), f32),
-        ),
-        (own_pair, fp, coupling, kl_lanes, stiff, int_slots, own_target),
+        jax.ShapeDtypeStruct((pairs, chaos, LANES), f32),
+        (fp, coupling, kl_lanes, stiff),
+    )
+    own_proj = call(
+        own_project_kernel,
+        jax.ShapeDtypeStruct((groups, chaos, LANES), f32),
+        (own_pair, fp, int_weave),
         1,
+        steps=steps,
+        split=(2,),
+        split_outs=(0,),
     )
     flux = call(
         flux_kernel,
@@ -327,19 +440,31 @@
     local_out = call(
         own_back_kernel,
         jax.ShapeDtypeStruct((pairs, chaos, LANES), f32),
-        (own_pair, flux, int_slots, own_target, local_out),
+        (own_pair, flux, int_weave, local_out),
         1,
+        steps=steps,
+        split=(1, 2),
     )
     result = call(
-        functools.partial(die_back_kernel, part=part, padded=padded),
-        jax.ShapeDtypeStruct((n_chaos * padded, nodes), bf16),
-        (die_pair, back_flux, die_slots, die_target, local_out),
+        functools.partial(die_back_kernel, part=part),
+        jax.ShapeDtypeStruct(sent.shape, bf16),
+        (die_pair, back_flux, die_weave, local_out),
         1,
-        (pltpu.VMEM((pairs, chaos, LANES), f32),),
-    )
-    result = result.reshape(n_chaos, padded, nodes)
+        (
+            pltpu.VMEM((pairs, chaos, LANES), f32),
+            pltpu.VMEM((n_chaos, 256, nodes // 16), bf16),
+        ),
+        steps=steps,
+        split=(1, 2),
+    )
     returned = lax.all_to_all(result, "chaos", split_axis=0, concat_axis=0, tiled=True)
-    return jnp.transpose(returned[:, :part], (1, 0, 2)).reshape(part, local_nodes)
+    return pl.pallas_call(
+        receive_kernel,
+        out_shape=jax.ShapeDtypeStruct((part, local_nodes), bf16),
+        grid=(n_chaos,),
+        in_specs=[pl.BlockSpec((1, 16 * part, nodes // 16), lambda c: (c, 0, 0))],
+        out_specs=pl.BlockSpec((part, nodes), lambda c: (0, c)),
+    )(returned)
 
 
 def solution(mesh):

time: 252 us -> 206 us (0.82)
  waiting for transfers between devices: 49.7 us -> 14.9 us
  local copies, waits for them, and re-layouts: 23.5 us -> 14 us
  blocking collectives: 42.6 us -> 38.6 us
  starting transfers between devices: 19.7 us -> 22.9 us
    all_to_all x1, waiting for transfers between devices: 34.2 us -> 0.01 us  [local(): lax.all_to_all(sent, 'chaos', split_axis=0, concat_axis=0, tiled=True)]
    all_to_all x1, waiting for transfers between devices: 6.56 us -> 0.01 us  [local(): meta = lax.all_to_all(meta, axes, split_axis=0, concat_axis=0, tiled=True)]
    all_to_all x2, waiting for transfers between devices: 8.92 us -> 14.9 us  [exchange(): lax.all_to_all(values, axes, split_axis=0, concat_axis=0, tiled=True)]
    unnamed x37, local copies, waits for them, and re-layouts: 7.17 us -> 2.33 us
    all_to_all x1, blocking collectives: 42.6 us -> 38.6 us  [local(): lax.all_to_all(result, 'chaos', split_axis=0, concat_axis=0, tiled=True)]
    all_to_all x1, starting transfers between devices: 3.71 us -> 6.46 us  [local(): lax.all_to_all(sent, 'chaos', split_axis=0, concat_axis=0, tiled=True)]
    pallas_call x6 -> x11, Pallas kernels: 99.3 us -> 99.7 us  [the longest x9 91.1 us: call(): pl.pallas_call(kernel, out_shape=shapes, grid=(steps,) if steps else (),...]
  transfers between devices with their start and end apart: 4 -> 4, of which waited for: 3 -> 2; matrix products, arithmetic and copies ran while one was open for 11% -> 13% of each run, Pallas kernels for 19% -> 34%
where the time goes in v2:
time: 206 us; the launch traced here: 205 us
  Pallas kernels  99.7 us (48%)
  blocking collectives  38.6 us (19%)
  starting transfers between devices  22.9 us (11%)
  waiting for transfers between devices  14.9 us (7%)
  local copies, waits for them, and re-layouts  14 us (7%)
  matrix products  8.95 us (4%)
  other arithmetic  5.24 us (3%)
    pallas_call x9, Pallas kernels, call(): pl.pallas_call(kernel, out_shape=shapes, grid=(steps,) if steps else (),...  91.1 us
    all_to_all x1, blocking collectives, local(): lax.all_to_all(result, 'chaos', split_axis=0, concat_axis=0, tiled=True)  38.6 us
    all_to_all x2, waiting for transfers between devices, exchange(): lax.all_to_all(values, axes, split_axis=0, concat_axis=0, tiled=True)  14.9 us
    all_to_all x2, starting transfers between devices, exchange(): lax.all_to_all(values, axes, split_axis=0, concat_axis=0, tiled=True)  10.2 us
    broadcast_in_dim x5, local copies, waits for them, and re-layouts, local(): jnp.where(on_diag, blocks, jnp.zeros((), bf16)).reshape(pairs, LANES, LANES)  7.39 us
    dot_general x1, matrix products, dense_coupling(): jnp.einsum('ta,tb->ab', left_hot, right_hot, precision=lax.Precision.HIGH...  6.91 us
    all_to_all x1, starting transfers between devices, local(): lax.all_to_all(sent, 'chaos', split_axis=0, concat_axis=0, tiled=True)  6.46 us
    all_to_all x1, starting transfers between devices, local(): meta = lax.all_to_all(meta, axes, split_axis=0, concat_axis=0, tiled=True)  6.24 us
  transfers between devices with their start and end apart: 4, of which 2 were waited for; matrix products, arithmetic and copies ran while one was open for 13% of the time, Pallas kernels for 34%

profile of v2, /device:TPU:0, one launch (start us, length us, event | category | flops | bytes accessed | tf_op | source)
XLA Modules:
  0.0 204.6 jit_solution(7303915320286394770)
XLA Ops:
  0.0 4.5 %shard_map.172 = bf16[4,672,256]{2,1,0:T(8,128)(2,1)} custom-call(bf16[42,16384]{1,0:T(8,128)(2,1)} %field_ref.1), custom_call_target="tpu_custom_call" | custom-call | tf_op jit(solution)/shard_map/pallas_call | solution.py:335
  4.5 6.5 %all-to-all-start = ((bf16[4,672,256]{2,1,0:T(8,128)(2,1)}), bf16[4,672,256]{2,1,0:T(8,128)(2,1)S(1)}, u32[]{:S(2)}, u32[]{:S(2)}) async-start(bf16[4,672,256]{2,1,0:T(8,128)(2,1)} %shard_map.172), calls=%async_computation | async-start | bytes 2752512 | tf_op jit(solution)/shard_map/all_to_all | solution.py:342
  12.5 2.0 shard_map.173
  16.5 6.9 %fusion.3 = bf16[1344,168]{0,1:T(8,128)(2,1)S(1)} fusion(s32[2688]{0:T(1024)S(1)} %multiply_add_fusion, f32[2688]{0:T(1024)S(1)} %copy-done.15, s32[2688]{0:T(1024)S(1)} %copy-done.16), kind=kOutput, calls=%fused_computation.5 | convolution fusion | flops 7287888384 | bytes 483840 | tf_op jit(solution)/shard_map/ta,tb->ab/dot_general | solution.py:277
  23.4 1.2 copy.89
  24.7 2.1 %broadcast_in_dim.80 = bf16[32,2,64,64]{3,2,1,0:T(8,128)(2,1)} reshape(bf16[64,4096]{1,0:T(8,128)(2,1)S(1)} %copy-done.4) | data formatting | bytes 1048576 | tf_op jit(solution)/shard_map/jit(_where)/broadcast_in_dim | solution.py:362
  26.7 3.3 %broadcast_in_dim.81 = bf16[32,2,64,2,64]{4,3,2,1,0:T(2,128)(2,1)S(1)} broadcast(bf16[32,2,64,64]{3,2,1,0:T(8,128)(2,1)} %broadcast_in_dim.80), dimensions={0,1,2,4} | broadcast | bytes 1572864 | tf_op jit(solution)/shard_map/jit(_where)/broadcast_in_dim | solution.py:362
  30.0 1.8 broadcast_in_dim.82
  32.7 13.2 %shard_map.174.weave_ref = bf16[32,128,1024]{2,1,0:T(8,128)(2,1)} custom-call(bf16[32,8,256]{2,1,0:T(8,128)(2,1)} %bitcast.41, s32[32,1,128]{2,1,0:T(1,128)} %bitcast.44), custom_call_target="tpu_custom_call" | custom-call | bytes 8536064 | tf_op jit(solution)/shard_map/pallas_call | solution.py:256
  48.6 6.2 %all-to-all-start.1 = ((bf16[32,8,384]{2,1,0:T(8,128)(2,1)}), bf16[32,8,384]{2,1,0:T(8,128)(2,1)S(1)}, u32[]{:S(2)}, u32[]{:S(2)}) async-start(bf16[32,8,384]{2,1,0:T(8,128)(2,1)} %bitcast.12), calls=%async_computation.1 | async-start | bytes 393216 | tf_op jit(solution)/shard_map/all_to_all | solution.py:378
  54.9 10.4 %shard_map.175 = (bf16[32,168,128]{2,1,0:T(8,128)(2,1)}, bf16[32,168,128]{2,1,0:T(8,128)(2,1)}) custom-call(s32[256]{0:T(256)} %and_select_fusion.3.pair_ref, bf16[4,672,256]{2,1,0:T(8,128)(2,1)} %copy-done, bf16[32,128,1024]{2,1,0:T(8,128)(2,1)} %shard_map.174.weave_ref), custom_call_target="tpu_custom_call" | custom-call | bytes 12518400 | tf_op jit(solution)/shard_map/pallas_call | solution.py:256
  65.3 5.7 %all-to-all-start.2 = ((bf16[32,168,128]{2,1,0:T(8,128)(2,1)}), bf16[32,168,128]{2,1,0:T(8,128)(2,1)S(1)}, u32[]{:S(2)}, u32[]{:S(2)}) async-start(bf16[32,168,128]{2,1,0:T(8,128)(2,1)} %get-tuple-element.27), calls=%async_computation.2 | async-start | bytes 2752512 | tf_op jit(solution)/shard_map/all_to_all | solution.py:398
  73.3 13.1 %shard_map.176.weave_ref = bf16[32,128,1024]{2,1,0:T(8,128)(2,1)} custom-call(bf16[32,8,256]{2,1,0:T(8,128)(2,1)} %slice_bitcast_fusion.1.mort_ref, s32[32,1,128]{2,1,0:T(1,128)} %bitcast.43), custom_call_target="tpu_custom_call" | custom-call | bytes 8536064 | tf_op jit(solution)/shard_map/pallas_call | solution.py:256
  87.0 9.5 %shard_map.177.own_ref = f32[32,168,128]{2,1,0:T(8,128)} custom-call(s32[256]{0:T(256)} %and_select_fusion.1.pair_ref, bf16[32,168,128]{2,1,0:T(8,128)(2,1)} %get-tuple-element.29.fp_ref, bf16[32,128,1024]{2,1,0:T(8,128)(2,1)} %shard_map.176.weave_ref), custom_call_target="tpu_custom_call" | custom-call | bytes 12518400 | tf_op jit(solution)/shard_map/pallas_call | solution.py:256
  97.5 5.3 %all-to-all-done.2.recv_ref = bf16[32,168,128]{2,1,0:T(8,128)(2,1)S(1)} async-done(((bf16[32,168,128]{2,1,0:T(8,128)(2,1)}), bf16[32,168,128]{2,1,0:T(8,128)(2,1)S(1)}, u32[]{:S(2)}, u32[]{:S(2)}) %all-to-all-start.2) | async-done | bytes 1376288 | tf_op jit(solution)/shard_map/all_to_all | solution.py:398
  102.8 1.1 copy-done.1
  103.9 9.1 %shard_map.178.flux_ref = bf16[32,168,128]{2,1,0:T(8,128)(2,1)} custom-call(bf16[32,168,128]{2,1,0:T(8,128)(2,1)} %copy-done.1, f32[32,168,128]{2,1,0:T(8,128)} %shard_map.177.own_ref, bf16[8,168,168]{2,1,0:T(8,128)(2,1)} %bitcast.34, f32[16,16,256]{2,1,0:T(8,128)} %fusion.15.coef_ref), custom_call_target="tpu_custom_call" | custom-call | bytes 6218752 | tf_op jit(solution)/shard_map/pallas_call | solution.py:256
  113.1 4.6 %all-to-all-start.3 = ((bf16[32,168,128]{2,1,0:T(8,128)(2,1)}), bf16[32,168,128]{2,1,0:T(8,128)(2,1)S(1)}, u32[]{:S(2)}, u32[]{:S(2)}) async-start(bf16[32,168,128]{2,1,0:T(8,128)(2,1)} %shard_map.178.flux_ref), calls=%async_computation.3 | async-start | bytes 2752512 | tf_op jit(solution)/shard_map/all_to_all | solution.py:398
  117.6 11.1 %shard_map.179.start_ref = f32[32,168,128]{2,1,0:T(8,128)} custom-call(bf16[32,168,128]{2,1,0:T(8,128)(2,1)} %get-tuple-element.29.fp_ref, bf16[8,168,168]{2,1,0:T(8,128)(2,1)} %bitcast.35, f32[16,16,256]{2,1,0:T(8,128)} %fusion.33.kl_ref, bf16[32,128,128]{2,1,0:T(8,128)(2,1)} %broadcast_select_fusion.stiff_ref), custom_call_target="tpu_custom_call" | custom-call | bytes 5891072 | tf_op jit(solution)/shard_map/pallas_call | solution.py:256
  128.8 11.2 %shard_map.180.start_ref = f32[32,168,128]{2,1,0:T(8,128)} custom-call(s32[256]{0:T(256)} %and_select_fusion.1.pair_ref, bf16[32,168,128]{2,1,0:T(8,128)(2,1)} %shard_map.178.flux_ref, bf16[32,128,1024]{2,1,0:T(8,128)(2,1)} %shard_map.176.weave_ref, f32[32,168,128]{2,1,0:T(8,128)} %shard_map.179.start_ref), custom_call_target="tpu_custom_call" | custom-call | bytes 15270912 | tf_op jit(solution)/shard_map/pallas_call | solution.py:256
  139.9 9.6 %all-to-all-done.3.flux_ref = bf16[32,168,128]{2,1,0:T(8,128)(2,1)S(1)} async-done(((bf16[32,168,128]{2,1,0:T(8,128)(2,1)}), bf16[32,168,128]{2,1,0:T(8,128)(2,1)S(1)}, u32[]{:S(2)}, u32[]{:S(2)}) %all-to-all-start.3) | async-done | bytes 1376288 | tf_op jit(solution)/shard_map/all_to_all | solution.py:398
  150.6 11.4 %shard_map.181 = bf16[4,672,256]{2,1,0:T(8,128)(2,1)} custom-call(s32[256]{0:T(256)} %and_select_fusion.3.pair_ref, bf16[32,168,128]{2,1,0:T(8,128)(2,1)} %copy-done.2, bf16[32,128,1024]{2,1,0:T(8,128)(2,1)} %shard_map.174.weave_ref, f32[32,168,128]{2,1,0:T(8,128)} %shard_map.180.start_ref), custom_call_target="tpu_custom_call" | custom-call | bytes 13894656 | tf_op jit(solution)/shard_map/pallas_call | solution.py:256
  162.0 38.6 %all_to_all.32.in_ref = bf16[4,672,256]{2,1,0:T(8,128)(2,1)} all-to-all(bf16[4,672,256]{2,1,0:T(8,128)(2,1)} %shard_map.181), channel_id=1, replica_groups=mesh['space'=8,'chaos'=4] {'chaos'}, dimensions={0} | all-to-all | bytes 2752512 | tf_op jit(solution)/shard_map/all_to_all | solution.py:460
  200.5 4.0 %shard_map.182 = bf16[42,16384]{1,0:T(8,128)(2,1)} custom-call(bf16[4,672,256]{2,1,0:T(8,128)(2,1)} %all_to_all.32.in_ref), custom_call_target="tpu_custom_call" | custom-call | tf_op jit(solution)/shard_map/pallas_call | solution.py:461
  (84 shorter events, 11.9 us)
Async XLA Ops:
  0.0 16.1 %copy-start.5 = (s32[6,16]{1,0:T(8,128)S(1)}, s32[6,16]{1,0:T(8,128)}, u32[]{:S(2)}) copy-start(s32[6,16]{1,0:T(8,128)} %constant.97.clone) | copy-start | bytes 1156
  0.0 11.0 %copy-start.10 = (s32[128]{0:T(128)S(1)}, s32[128]{0:T(128)}, u32[]{:S(2)}) copy-start(s32[128]{0:T(128)} %param.27) | copy-start | bytes 1540
  0.0 11.7 %copy-start.17 = (s32[128]{0:T(128)S(1)}, s32[128]{0:T(128)}, u32[]{:S(2)}) copy-start(s32[128]{0:T(128)} %param.28) | copy-start | bytes 1540
  0.0 11.7 %copy-start.11 = (s32[128]{0:T(128)S(1)}, s32[128]{0:T(128)}, u32[]{:S(2)}) copy-start(s32[128]{0:T(128)} %param.26) | copy-start | bytes 1540
  0.0 11.7 %copy-start.12 = (s32[128]{0:T(128)S(1)}, s32[128]{0:T(128)}, u32[]{:S(2)}) copy-start(s32[128]{0:T(128)} %param.25) | copy-start | bytes 1540
  0.0 11.8 %copy-start.9 = (bf16[128,9]{0,1:T(8,128)(2,1)S(1)}, bf16[128,9]{0,1:T(8,128)(2,1)}, u32[]{:S(2)}) copy-start(bf16[128,9]{0,1:T(8,128)(2,1)} %param.31) | copy-start | bytes 6916
  4.5 11.9 %copy-start.6 = (s32[2688]{0:T(1024)S(1)}, s32[2688]{0:T(1024)}, u32[]{:S(2)}) copy-start(s32[2688]{0:T(1024)} %param.22) | copy-start | bytes 32260
  4.5 11.9 %copy-start.7 = (s32[2688]{0:T(1024)S(1)}, s32[2688]{0:T(1024)}, u32[]{:S(2)}) copy-start(s32[2688]{0:T(1024)} %param.21) | copy-start | bytes 32260
  4.5 11.9 %copy-start.15 = (f32[2688]{0:T(1024)S(1)}, f32[2688]{0:T(1024)}, u32[]{:S(2)}) copy-start(f32[2688]{0:T(1024)} %param.24) | copy-start | bytes 32260
  4.5 11.9 %copy-start.16 = (s32[2688]{0:T(1024)S(1)}, s32[2688]{0:T(1024)}, u32[]{:S(2)}) copy-start(s32[2688]{0:T(1024)} %param.23) | copy-start | bytes 32260
  4.5 44.1 %all-to-all-start = ((bf16[4,672,256]{2,1,0:T(8,128)(2,1)}), bf16[4,672,256]{2,1,0:T(8,128)(2,1)S(1)}, u32[]{:S(2)}, u32[]{:S(2)}) async-start(bf16[4,672,256]{2,1,0:T(8,128)(2,1)} %shard_map.172), calls=%async_computation | async-start | bytes 2752512 | tf_op jit(solution)/shard_map/all_to_all | solution.py:342
  16.4 8.1 %copy-start.8 = (f32[9,64]{1,0:T(8,128)S(1)}, f32[9,64]{1,0:T(8,128)}, u32[]{:S(2)}) copy-start(f32[9,64]{1,0:T(8,128)} %param.20) | copy-start | bytes 6916
  16.4 8.2 %copy-start.4 = (bf16[64,4096]{1,0:T(8,128)(2,1)S(1)}, bf16[64,4096]{1,0:T(8,128)(2,1)}, u32[]{:S(2)}) copy-start(bf16[64,4096]{1,0:T(8,128)(2,1)} %param.19) | copy-start | bytes 1572868
  32.7 14.9 %copy-start.3 = (bf16[32,128,128]{2,1,0:T(8,128)(2,1)S(1)}, bf16[32,128,128]{2,1,0:T(8,128)(2,1)}, u32[]{:S(2)}) copy-start(bf16[32,128,128]{2,1,0:T(8,128)(2,1)} %broadcast_in_dim.82) | copy-start | bytes 3145732
  48.6 6.3 %copy-start = (bf16[4,672,256]{2,1,0:T(8,128)(2,1)}, bf16[4,672,256]{2,1,0:T(8,128)(2,1)S(1)}, u32[]{:S(2)}) copy-start(bf16[4,672,256]{2,1,0:T(8,128)(2,1)S(1)} %all-to-all-done.wide_ref) | copy-start | bytes 4128772
  48.6 16.7 %all-to-all-start.1 = ((bf16[32,8,384]{2,1,0:T(8,128)(2,1)}), bf16[32,8,384]{2,1,0:T(8,128)(2,1)S(1)}, u32[]{:S(2)}, u32[]{:S(2)}) async-start(bf16[32,8,384]{2,1,0:T(8,128)(2,1)} %bitcast.12), calls=%async_computation.1 | async-start | bytes 393216 | tf_op jit(solution)/shard_map/all_to_all | solution.py:378
  65.3 5.9 %copy-start.13 = (s32[64]{0:T(128)S(1)}, s32[64]{0:T(128)}, u32[]{:S(2)}) copy-start(s32[64]{0:T(128)} %param.33) | copy-start | bytes 772
  65.3 5.9 %copy-start.14 = (s32[64]{0:T(128)S(1)}, s32[64]{0:T(128)}, u32[]{:S(2)}) copy-start(s32[64]{0:T(128)} %param.32) | copy-start | bytes 772
  65.3 37.5 %all-to-all-start.2 = ((bf16[32,168,128]{2,1,0:T(8,128)(2,1)}), bf16[32,168,128]{2,1,0:T(8,128)(2,1)S(1)}, u32[]{:S(2)}, u32[]{:S(2)}) async-start(bf16[32,168,128]{2,1,0:T(8,128)(2,1)} %get-tuple-element.27), calls=%async_computation.2 | async-start | bytes 2752512 | tf_op jit(solution)/shard_map/all_to_all | solution.py:398
  102.8 1.1 copy-start.1
  113.1 36.4 %all-to-all-start.3 = ((bf16[32,168,128]{2,1,0:T(8,128)(2,1)}), bf16[32,168,128]{2,1,0:T(8,128)(2,1)S(1)}, u32[]{:S(2)}, u32[]{:S(2)}) async-start(bf16[32,168,128]{2,1,0:T(8,128)(2,1)} %shard_map.178.flux_ref), calls=%async_computation.3 | async-start | bytes 2752512 | tf_op jit(solution)/shard_map/all_to_all | solution.py:398
  149.5 1.1 copy-start.2

commit v3 on v2

--- a/solution.py
+++ b/solution.py
@@ -356,11 +356,6 @@
     die_pair, die_target = slot_targets(die_ids[:, 0], die_ids[:, 1])
 
     coupling = dense_coupling(triple_mode, triple_row, triple_col, triple_value, modes, chaos)
-    kl_lanes = lane_weights(kl_coef, ELEM_NODES)
-    blocks = stiffness.reshape(pairs, 2, ELEM_NODES, 1, ELEM_NODES)
-    on_diag = jnp.eye(2, dtype=bool)[None, :, None, :, None]
-    stiff = jnp.where(on_diag, blocks, jnp.zeros((), bf16)).reshape(pairs, LANES, LANES)
-
     groups3 = (groups, 8, 256)
     weave_shape = jax.ShapeDtypeStruct((groups, LANES, 8 * LANES), bf16)
     steps = groups // 4
@@ -372,8 +367,8 @@
         split=(0, 1),
         split_outs=(0,),
     )
-    wide, meta, die_weave, die_pair, coupling, kl_lanes, stiff = lax.optimization_barrier(
-        (wide, meta, die_weave, die_pair, coupling, kl_lanes, stiff)
+    wide, meta, die_weave, die_pair, coupling = lax.optimization_barrier(
+        (wide, meta, die_weave, die_pair, coupling)
     )
     meta = lax.all_to_all(meta, axes, split_axis=0, concat_axis=0, tiled=True)
     fp, proj = call(
@@ -417,11 +412,6 @@
         split=(0, 1),
         split_outs=(0,),
     )
-    local_out = call(
-        element_kernel,
-        jax.ShapeDtypeStruct((pairs, chaos, LANES), f32),
-        (fp, coupling, kl_lanes, stiff),
-    )
     own_proj = call(
         own_project_kernel,
         jax.ShapeDtypeStruct((groups, chaos, LANES), f32),
@@ -436,7 +426,17 @@
         jax.ShapeDtypeStruct((groups, chaos, LANES), bf16),
         (recv, own_proj, coupling, coef_lanes),
     )
+    flux, stiffness, kl_coef = lax.optimization_barrier((flux, stiffness, kl_coef))
     back_flux = exchange(flux)
+    kl_lanes = lane_weights(kl_coef, ELEM_NODES)
+    blocks = stiffness.reshape(pairs, 2, ELEM_NODES, 1, ELEM_NODES)
+    on_diag = jnp.eye(2, dtype=bool)[None, :, None, :, None]
+    stiff = jnp.where(on_diag, blocks, jnp.zeros((), bf16)).reshape(pairs, LANES, LANES)
+    local_out = call(
+        element_kernel,
+        jax.ShapeDtypeStruct((pairs, chaos, LANES), f32),
+        (fp, coupling, kl_lanes, stiff),
+    )
     local_out = call(
         own_back_kernel,
         jax.ShapeDtypeStruct((pairs, chaos, LANES), f32),

time: 206 us -> 200 us (0.971)
  waiting for transfers between devices: 14.9 us -> 10.1 us
  starting transfers between devices: 22.9 us -> 20.7 us
    all_to_all x2, waiting for transfers between devices: 14.9 us -> 5.19 us  [exchange(): lax.all_to_all(values, axes, split_axis=0, concat_axis=0, tiled=True)]
    all_to_all x1, waiting for transfers between devices: 0.01 us -> 4.93 us  [local(): lax.all_to_all(sent, 'chaos', split_axis=0, concat_axis=0, tiled=True)]
    all_to_all x1, starting transfers between devices: 6.24 us -> 3.71 us  [local(): meta = lax.all_to_all(meta, axes, split_axis=0, concat_axis=0, tiled=True)]
  transfers between devices with their start and end apart: 4 -> 4, of which waited for: 2 -> 2; matrix products, arithmetic and copies ran while one was open for 13% -> 14% of each run, Pallas kernels for 34% -> 36%
where the time goes in v3:
time: 200 us; the launch traced here: 198 us
  Pallas kernels  99.5 us (50%)
  blocking collectives  38 us (19%)
  starting transfers between devices  20.7 us (10%)
  local copies, waits for them, and re-layouts  14 us (7%)
  waiting for transfers between devices  10.1 us (5%)
  matrix products  8.91 us (4%)
  other arithmetic  6.43 us (3%)
    pallas_call x9, Pallas kernels, call(): pl.pallas_call(kernel, out_shape=shapes, grid=(steps,) if steps else (),...  91 us
    all_to_all x1, blocking collectives, local(): lax.all_to_all(result, 'chaos', split_axis=0, concat_axis=0, tiled=True)  38 us
    all_to_all x2, starting transfers between devices, exchange(): lax.all_to_all(values, axes, split_axis=0, concat_axis=0, tiled=True)  10.6 us
    broadcast_in_dim x5, local copies, waits for them, and re-layouts, local(): jnp.where(on_diag, blocks, jnp.zeros((), bf16)).reshape(pairs, LANES, LANES)  7.37 us
    dot_general x1, matrix products, dense_coupling(): jnp.einsum('ta,tb->ab', left_hot, right_hot, precision=lax.Precision.HIGH...  6.91 us
    all_to_all x1, starting transfers between devices, local(): lax.all_to_all(sent, 'chaos', split_axis=0, concat_axis=0, tiled=True)  6.46 us
    all_to_all x2, waiting for transfers between devices, exchange(): lax.all_to_all(values, axes, split_axis=0, concat_axis=0, tiled=True)  5.19 us
    all_to_all x1, waiting for transfers between devices, local(): lax.all_to_all(sent, 'chaos', split_axis=0, concat_axis=0, tiled=True)  4.93 us
  transfers between devices with their start and end apart: 4, of which 2 were waited for; matrix products, arithmetic and copies ran while one was open for 14% of the time, Pallas kernels for 36%

profile of v3, /device:TPU:0, one launch (start us, length us, event | category | flops | bytes accessed | tf_op | source)
XLA Modules:
  0.0 198.1 jit_solution(2686896206816429078)
XLA Ops:
  0.0 4.5 %shard_map.172 = bf16[4,672,256]{2,1,0:T(8,128)(2,1)} custom-call(bf16[42,16384]{1,0:T(8,128)(2,1)} %field_ref.1), custom_call_target="tpu_custom_call" | custom-call | tf_op jit(solution)/shard_map/pallas_call | solution.py:335
  4.5 6.5 %all-to-all-start = ((bf16[4,672,256]{2,1,0:T(8,128)(2,1)}), bf16[4,672,256]{2,1,0:T(8,128)(2,1)S(1)}, u32[]{:S(2)}, u32[]{:S(2)}) async-start(bf16[4,672,256]{2,1,0:T(8,128)(2,1)} %shard_map.172), calls=%async_computation | async-start | bytes 2752512 | tf_op jit(solution)/shard_map/all_to_all | solution.py:342
  12.6 2.0 shard_map.173
  16.4 6.9 %fusion.3 = bf16[1344,168]{0,1:T(8,128)(2,1)S(1)} fusion(s32[2688]{0:T(1024)S(1)} %multiply_add_fusion, f32[2688]{0:T(1024)S(1)} %copy-done.14, s32[2688]{0:T(1024)S(1)} %copy-done.15), kind=kOutput, calls=%fused_computation.5 | convolution fusion | flops 7287888384 | bytes 483840 | tf_op jit(solution)/shard_map/ta,tb->ab/dot_general | solution.py:277
  23.3 1.2 copy.89
  25.1 13.1 %shard_map.174.weave_ref = bf16[32,128,1024]{2,1,0:T(8,128)(2,1)} custom-call(bf16[32,8,256]{2,1,0:T(8,128)(2,1)} %bitcast.41, s32[32,1,128]{2,1,0:T(1,128)} %bitcast.44), custom_call_target="tpu_custom_call" | custom-call | bytes 8536064 | tf_op jit(solution)/shard_map/pallas_call | solution.py:256
  38.8 4.9 %all-to-all-done.wide_ref = bf16[4,672,256]{2,1,0:T(8,128)(2,1)S(1)} async-done(((bf16[4,672,256]{2,1,0:T(8,128)(2,1)}), bf16[4,672,256]{2,1,0:T(8,128)(2,1)S(1)}, u32[]{:S(2)}, u32[]{:S(2)}) %all-to-all-start) | async-done | bytes 1376288 | tf_op jit(solution)/shard_map/all_to_all | solution.py:342
  43.7 3.7 %all-to-all-start.1 = ((bf16[32,8,384]{2,1,0:T(8,128)(2,1)}), bf16[32,8,384]{2,1,0:T(8,128)(2,1)S(1)}, u32[]{:S(2)}, u32[]{:S(2)}) async-start(bf16[32,8,384]{2,1,0:T(8,128)(2,1)} %bitcast.9), calls=%async_computation.1 | async-start | bytes 393216 | tf_op jit(solution)/shard_map/all_to_all | solution.py:373
  47.5 10.4 %shard_map.175 = (bf16[32,168,128]{2,1,0:T(8,128)(2,1)}, bf16[32,168,128]{2,1,0:T(8,128)(2,1)}) custom-call(s32[256]{0:T(256)} %and_select_fusion.3.pair_ref, bf16[4,672,256]{2,1,0:T(8,128)(2,1)} %copy-done, bf16[32,128,1024]{2,1,0:T(8,128)(2,1)} %shard_map.174.weave_ref), custom_call_target="tpu_custom_call" | custom-call | bytes 12518400 | tf_op jit(solution)/shard_map/pallas_call | solution.py:256
  57.9 6.0 %all-to-all-start.2 = ((bf16[32,168,128]{2,1,0:T(8,128)(2,1)}), bf16[32,168,128]{2,1,0:T(8,128)(2,1)S(1)}, u32[]{:S(2)}, u32[]{:S(2)}) async-start(bf16[32,168,128]{2,1,0:T(8,128)(2,1)} %get-tuple-element.28), calls=%async_computation.2 | async-start | bytes 2752512 | tf_op jit(solution)/shard_map/all_to_all | solution.py:393
  66.2 13.1 %shard_map.176.weave_ref = bf16[32,128,1024]{2,1,0:T(8,128)(2,1)} custom-call(bf16[32,8,256]{2,1,0:T(8,128)(2,1)} %slice_bitcast_fusion.1.mort_ref, s32[32,1,128]{2,1,0:T(1,128)} %bitcast.43), custom_call_target="tpu_custom_call" | custom-call | bytes 8536064 | tf_op jit(solution)/shard_map/pallas_call | solution.py:256
  79.9 9.5 %shard_map.177.own_ref = f32[32,168,128]{2,1,0:T(8,128)} custom-call(s32[256]{0:T(256)} %and_select_fusion.2.pair_ref, bf16[32,168,128]{2,1,0:T(8,128)(2,1)} %get-tuple-element.30.fp_ref, bf16[32,128,1024]{2,1,0:T(8,128)(2,1)} %shard_map.176.weave_ref), custom_call_target="tpu_custom_call" | custom-call | bytes 12518400 | tf_op jit(solution)/shard_map/pallas_call | solution.py:256
  90.4 5.2 %all-to-all-done.2.recv_ref = bf16[32,168,128]{2,1,0:T(8,128)(2,1)S(1)} async-done(((bf16[32,168,128]{2,1,0:T(8,128)(2,1)}), bf16[32,168,128]{2,1,0:T(8,128)(2,1)S(1)}, u32[]{:S(2)}, u32[]{:S(2)}) %all-to-all-start.2) | async-done | bytes 1376288 | tf_op jit(solution)/shard_map/all_to_all | solution.py:393
  96.7 9.1 %shard_map.178.flux_ref = bf16[32,168,128]{2,1,0:T(8,128)(2,1)} custom-call(bf16[32,168,128]{2,1,0:T(8,128)(2,1)} %copy-done.1, f32[32,168,128]{2,1,0:T(8,128)} %shard_map.177.own_ref, bf16[8,168,168]{2,1,0:T(8,128)(2,1)} %bitcast.34, f32[16,16,256]{2,1,0:T(8,128)} %fusion.15.coef_ref), custom_call_target="tpu_custom_call" | custom-call | bytes 6218752 | tf_op jit(solution)/shard_map/pallas_call | solution.py:256
  105.8 4.6 %all-to-all-start.3 = ((bf16[32,168,128]{2,1,0:T(8,128)(2,1)}), bf16[32,168,128]{2,1,0:T(8,128)(2,1)S(1)}, u32[]{:S(2)}, u32[]{:S(2)}) async-start(bf16[32,168,128]{2,1,0:T(8,128)(2,1)} %shard_map.178.flux_ref), calls=%async_computation.3 | async-start | bytes 2752512 | tf_op jit(solution)/shard_map/all_to_all | solution.py:393
  110.6 2.1 %broadcast_in_dim.83 = bf16[32,2,64,64]{3,2,1,0:T(8,128)(2,1)} reshape(bf16[64,4096]{1,0:T(8,128)(2,1)S(1)} %copy-done.3) | data formatting | bytes 1048576 | tf_op jit(solution)/shard_map/jit(_where)/broadcast_in_dim | solution.py:434
  112.7 3.3 %broadcast_in_dim.84 = bf16[32,2,64,2,64]{4,3,2,1,0:T(2,128)(2,1)S(1)} broadcast(bf16[32,2,64,64]{3,2,1,0:T(8,128)(2,1)} %broadcast_in_dim.83), dimensions={0,1,2,4} | broadcast | bytes 1572864 | tf_op jit(solution)/shard_map/jit(_where)/broadcast_in_dim | solution.py:434
  116.0 1.8 broadcast_in_dim.85
  118.9 2.3 %broadcast_select_fusion.stiff_ref = bf16[32,128,128]{2,1,0:T(8,128)(2,1)} fusion(bf16[32,128,128]{2,1,0:T(8,128)(2,1)} %broadcast_in_dim.85, pred[128,128]{1,0:T(8,128)(4,1)S(1)} %broadcast_in_dim.81), kind=kLoop, calls=%fused_computation.9 | loop fusion | flops 524288 | bytes 2113536 | tf_op jit(solution)/shard_map/jit(_where)/select_n | solution.py:434
  121.2 11.2 %shard_map.179.start_ref = f32[32,168,128]{2,1,0:T(8,128)} custom-call(bf16[32,168,128]{2,1,0:T(8,128)(2,1)} %get-tuple-element.30.fp_ref, bf16[8,168,168]{2,1,0:T(8,128)(2,1)} %bitcast.35, f32[16,16,256]{2,1,0:T(8,128)} %fusion.33.kl_ref, bf16[32,128,128]{2,1,0:T(8,128)(2,1)} %broadcast_select_fusion.stiff_ref), custom_call_target="tpu_custom_call" | custom-call | bytes 5891072 | tf_op jit(solution)/shard_map/pallas_call | solution.py:256
  132.4 11.1 %shard_map.180.start_ref = f32[32,168,128]{2,1,0:T(8,128)} custom-call(s32[256]{0:T(256)} %and_select_fusion.2.pair_ref, bf16[32,168,128]{2,1,0:T(8,128)(2,1)} %shard_map.178.flux_ref, bf16[32,128,1024]{2,1,0:T(8,128)(2,1)} %shard_map.176.weave_ref, f32[32,168,128]{2,1,0:T(8,128)} %shard_map.179.start_ref), custom_call_target="tpu_custom_call" | custom-call | bytes 15270912 | tf_op jit(solution)/shard_map/pallas_call | solution.py:256
  144.6 11.4 %shard_map.181 = bf16[4,672,256]{2,1,0:T(8,128)(2,1)} custom-call(s32[256]{0:T(256)} %and_select_fusion.3.pair_ref, bf16[32,168,128]{2,1,0:T(8,128)(2,1)} %copy-done.2, bf16[32,128,1024]{2,1,0:T(8,128)(2,1)} %shard_map.174.weave_ref, f32[32,168,128]{2,1,0:T(8,128)} %shard_map.180.start_ref), custom_call_target="tpu_custom_call" | custom-call | bytes 13894656 | tf_op jit(solution)/shard_map/pallas_call | solution.py:256
  156.0 38.0 %all_to_all.32.in_ref = bf16[4,672,256]{2,1,0:T(8,128)(2,1)} all-to-all(bf16[4,672,256]{2,1,0:T(8,128)(2,1)} %shard_map.181), channel_id=1, replica_groups=mesh['space'=8,'chaos'=4] {'chaos'}, dimensions={0} | all-to-all | bytes 2752512 | tf_op jit(solution)/shard_map/all_to_all | solution.py:460
  194.0 4.0 %shard_map.182 = bf16[42,16384]{1,0:T(8,128)(2,1)} custom-call(bf16[4,672,256]{2,1,0:T(8,128)(2,1)} %all_to_all.32.in_ref), custom_call_target="tpu_custom_call" | custom-call | tf_op jit(solution)/shard_map/pallas_call | solution.py:461
  (82 shorter events, 11.8 us)
Async XLA Ops:
  0.0 15.8 %copy-start.4 = (s32[6,16]{1,0:T(8,128)S(1)}, s32[6,16]{1,0:T(8,128)}, u32[]{:S(2)}) copy-start(s32[6,16]{1,0:T(8,128)} %constant.97.clone) | copy-start | bytes 1156
  0.0 11.0 %copy-start.16 = (s32[128]{0:T(128)S(1)}, s32[128]{0:T(128)}, u32[]{:S(2)}) copy-start(s32[128]{0:T(128)} %param.28) | copy-start | bytes 1540
  0.0 11.0 %copy-start.11 = (s32[128]{0:T(128)S(1)}, s32[128]{0:T(128)}, u32[]{:S(2)}) copy-start(s32[128]{0:T(128)} %param.25) | copy-start | bytes 1540
  0.0 11.0 %copy-start.10 = (s32[128]{0:T(128)S(1)}, s32[128]{0:T(128)}, u32[]{:S(2)}) copy-start(s32[128]{0:T(128)} %param.26) | copy-start | bytes 1540
  0.0 11.0 %copy-start.8 = (bf16[128,9]{0,1:T(8,128)(2,1)S(1)}, bf16[128,9]{0,1:T(8,128)(2,1)}, u32[]{:S(2)}) copy-start(bf16[128,9]{0,1:T(8,128)(2,1)} %param.31) | copy-start | bytes 6916
  0.0 11.2 %copy-start.9 = (s32[128]{0:T(128)S(1)}, s32[128]{0:T(128)}, u32[]{:S(2)}) copy-start(s32[128]{0:T(128)} %param.27) | copy-start | bytes 1540
  4.5 11.8 %copy-start.5 = (s32[2688]{0:T(1024)S(1)}, s32[2688]{0:T(1024)}, u32[]{:S(2)}) copy-start(s32[2688]{0:T(1024)} %param.22) | copy-start | bytes 32260
  4.5 11.8 %copy-start.6 = (s32[2688]{0:T(1024)S(1)}, s32[2688]{0:T(1024)}, u32[]{:S(2)}) copy-start(s32[2688]{0:T(1024)} %param.21) | copy-start | bytes 32260
  4.5 11.8 %copy-start.14 = (f32[2688]{0:T(1024)S(1)}, f32[2688]{0:T(1024)}, u32[]{:S(2)}) copy-start(f32[2688]{0:T(1024)} %param.24) | copy-start | bytes 32260
  4.5 11.9 %copy-start.15 = (s32[2688]{0:T(1024)S(1)}, s32[2688]{0:T(1024)}, u32[]{:S(2)}) copy-start(s32[2688]{0:T(1024)} %param.23) | copy-start | bytes 32260
  4.5 39.2 %all-to-all-start = ((bf16[4,672,256]{2,1,0:T(8,128)(2,1)}), bf16[4,672,256]{2,1,0:T(8,128)(2,1)S(1)}, u32[]{:S(2)}, u32[]{:S(2)}) async-start(bf16[4,672,256]{2,1,0:T(8,128)(2,1)} %shard_map.172), calls=%async_computation | async-start | bytes 2752512 | tf_op jit(solution)/shard_map/all_to_all | solution.py:342
  43.7 3.7 %copy-start = (bf16[4,672,256]{2,1,0:T(8,128)(2,1)}, bf16[4,672,256]{2,1,0:T(8,128)(2,1)S(1)}, u32[]{:S(2)}) copy-start(bf16[4,672,256]{2,1,0:T(8,128)(2,1)S(1)} %all-to-all-done.wide_ref) | copy-start | bytes 4128772
  43.7 14.1 %all-to-all-start.1 = ((bf16[32,8,384]{2,1,0:T(8,128)(2,1)}), bf16[32,8,384]{2,1,0:T(8,128)(2,1)S(1)}, u32[]{:S(2)}, u32[]{:S(2)}) async-start(bf16[32,8,384]{2,1,0:T(8,128)(2,1)} %bitcast.9), calls=%async_computation.1 | async-start | bytes 393216 | tf_op jit(solution)/shard_map/all_to_all | solution.py:373
  57.9 6.2 %copy-start.12 = (s32[64]{0:T(128)S(1)}, s32[64]{0:T(128)}, u32[]{:S(2)}) copy-start(s32[64]{0:T(128)} %param.33) | copy-start | bytes 772
  57.9 6.2 %copy-start.13 = (s32[64]{0:T(128)S(1)}, s32[64]{0:T(128)}, u32[]{:S(2)}) copy-start(s32[64]{0:T(128)} %param.32) | copy-start | bytes 772
  57.9 37.7 %all-to-all-start.2 = ((bf16[32,168,128]{2,1,0:T(8,128)(2,1)}), bf16[32,168,128]{2,1,0:T(8,128)(2,1)S(1)}, u32[]{:S(2)}, u32[]{:S(2)}) async-start(bf16[32,168,128]{2,1,0:T(8,128)(2,1)} %get-tuple-element.28), calls=%async_computation.2 | async-start | bytes 2752512 | tf_op jit(solution)/shard_map/all_to_all | solution.py:393
  95.6 1.1 copy-start.1
  105.8 4.8 %copy-start.3 = (bf16[64,4096]{1,0:T(8,128)(2,1)S(1)}, bf16[64,4096]{1,0:T(8,128)(2,1)}, u32[]{:S(2)}) copy-start(bf16[64,4096]{1,0:T(8,128)(2,1)} %param.19) | copy-start | bytes 1572868
  105.8 37.7 %all-to-all-start.3 = ((bf16[32,168,128]{2,1,0:T(8,128)(2,1)}), bf16[32,168,128]{2,1,0:T(8,128)(2,1)S(1)}, u32[]{:S(2)}, u32[]{:S(2)}) async-start(bf16[32,168,128]{2,1,0:T(8,128)(2,1)} %shard_map.178.flux_ref), calls=%async_computation.3 | async-start | bytes 2752512 | tf_op jit(solution)/shard_map/all_to_all | solution.py:393
  112.7 5.1 %copy-start.7 = (f32[9,64]{1,0:T(8,128)S(1)}, f32[9,64]{1,0:T(8,128)}, u32[]{:S(2)}) copy-start(f32[9,64]{1,0:T(8,128)} %param.20) | copy-start | bytes 6916
  143.5 1.1 copy-start.2
